TPU v7x, 32 devices: a whole 2x2x4 slice. The times are simulated.
32 devices in a mesh: dp: 16 (over z, y, x), hid: 2 (over core).
Axes of the slice: x: 2, y: 2, z: 4, core: 2. Of those that a mesh axis runs over, the one named last changes fastest.
Arguments:
- field_ids: int32 [32768, 26, 4], P('dp'), may hold values from 0 to 255
- bag_lengths: int32 [32768, 26], P('dp'), may hold values from 1 to 4
- dense_values: float32 [32768, 13], P('dp'), may hold values from -12 to 12
- labels: int32 [32768, 2], P('dp'), may hold values from 0 to 1
- tables: float32 [26, 256, 16], replicated, may hold values from -1.5 to 1.5
- tables_momentum: float32 [26, 256, 16], replicated, may hold values from -0.625 to 0.625
- tables_average: float32 [26, 256, 16], replicated, may hold values from -1.5 to 1.5
- in_weight: float32 [429, 512], replicated, may hold values from -0.3125 to 0.3125
- in_weight_momentum: float32 [429, 512], replicated, may hold values from -0.625 to 0.625
- in_weight_average: float32 [429, 512], replicated, may hold values from -0.3125 to 0.3125
- expert_up: float32 [4, 512, 256], P(None, None, 'hid'), may hold values from -0.25 to 0.25
- expert_up_momentum: float32 [4, 512, 256], P(None, None, 'hid'), may hold values from -0.625 to 0.625
- expert_up_average: float32 [4, 512, 256], P(None, None, 'hid'), may hold values from -0.25 to 0.25
- expert_down: float32 [4, 256, 128], P(None, 'hid'), may hold values from -0.375 to 0.375
- expert_down_momentum: float32 [4, 256, 128], P(None, 'hid'), may hold values from -0.625 to 0.625
- expert_down_average: float32 [4, 256, 128], P(None, 'hid'), may hold values from -0.375 to 0.375
- expert_up_bias: float32 [4, 256], P(None, 'hid'), may hold values from -0.625 to 0.625
- expert_up_bias_momentum: float32 [4, 256], P(None, 'hid'), may hold values from -0.625 to 0.625
- expert_up_bias_average: float32 [4, 256], P(None, 'hid'), may hold values from -0.625 to 0.625
- gate_weight: float32 [2, 512, 4], replicated, may hold values from -0.125 to 0.125
- gate_weight_momentum: float32 [2, 512, 4], replicated, may hold values from -0.625 to 0.625
- gate_weight_average: float32 [2, 512, 4], replicated, may hold values from -0.125 to 0.125
- tower_up: float32 [2, 128, 64], replicated, may hold values from -0.5 to 0.5
- tower_up_momentum: float32 [2, 128, 64], replicated, may hold values from -0.625 to 0.625
- tower_up_average: float32 [2, 128, 64], replicated, may hold values from -0.5 to 0.5
- tower_out: float32 [2, 64], replicated, may hold values from -0.75 to 0.75
- tower_out_momentum: float32 [2, 64], replicated, may hold values from -0.625 to 0.625
- tower_out_average: float32 [2, 64], replicated, may hold values from -0.75 to 0.75
- biases: float32 [1162], replicated, may hold values from -0.625 to 0.625
- biases_momentum: float32 [1162], replicated, may hold values from -0.625 to 0.625
- biases_average: float32 [1162], replicated, may hold values from -0.625 to 0.625
Outputs:
- new_tables: float32 [26, 256, 16], replicated
- new_tables_momentum: float32 [26, 256, 16], replicated
- new_tables_average: float32 [26, 256, 16], replicated
- tables_rounded: bfloat16 [26, 256, 16], replicated
- new_in_weight: float32 [429, 512], replicated
- new_in_weight_momentum: float32 [429, 512], replicated
- new_in_weight_average: float32 [429, 512], replicated
- in_weight_rounded: bfloat16 [429, 512], replicated
- new_expert_up: float32 [4, 512, 256], P(None, None, 'hid')
- new_expert_up_momentum: float32 [4, 512, 256], P(None, None, 'hid')
- new_expert_up_average: float32 [4, 512, 256], P(None, None, 'hid')
- expert_up_rounded: bfloat16 [4, 512, 256], P(None, None, 'hid')
- new_expert_down: float32 [4, 256, 128], P(None, 'hid')
- new_expert_down_momentum: float32 [4, 256, 128], P(None, 'hid')
- new_expert_down_average: float32 [4, 256, 128], P(None, 'hid')
- expert_down_rounded: bfloat16 [4, 256, 128], P(None, 'hid')
- new_expert_up_bias: float32 [4, 256], P(None, 'hid')
- new_expert_up_bias_momentum: float32 [4, 256], P(None, 'hid')
- new_expert_up_bias_average: float32 [4, 256], P(None, 'hid')
- expert_up_bias_rounded: bfloat16 [4, 256], P(None, 'hid')
- new_gate_weight: float32 [2, 512, 4], replicated
- new_gate_weight_momentum: float32 [2, 512, 4], replicated
- new_gate_weight_average: float32 [2, 512, 4], replicated
- gate_weight_rounded: bfloat16 [2, 512, 4], replicated
- new_tower_up: float32 [2, 128, 64], replicated
- new_tower_up_momentum: float32 [2, 128, 64], replicated
- new_tower_up_average: float32 [2, 128, 64], replicated
- tower_up_rounded: bfloat16 [2, 128, 64], replicated
- new_tower_out: float32 [2, 64], replicated
- new_tower_out_momentum: float32 [2, 64], replicated
- new_tower_out_average: float32 [2, 64], replicated
- tower_out_rounded: bfloat16 [2, 64], replicated
- new_biases: float32 [1162], replicated
- new_biases_momentum: float32 [1162], replicated
- new_biases_average: float32 [1162], replicated
- biases_rounded: bfloat16 [1162], replicated
- layer_rms: float32 [4], replicated
All inputs are finite; a program needn't handle non-finite values.
Results may differ from a plain program's by a relative error of at most 0.001.
Values sent between devices are 32-bit elements; how exact they have to be, the bound alone decides.
A program may use at most 128 MiB of HBM per device.

v0:
```python
import functools

import jax
import jax.numpy as jnp
from jax import lax
from jax.experimental import pallas as pl
from jax.experimental.pallas import tpu as pltpu
from jax.sharding import PartitionSpec as P

D = 512
HID = 256
OUT = 128
TH = 64
TASKS = 2
EXPERTS = 4
FIELDS = 26
VOCAB = 256
EMB = 16
POOLED = 416
IN_ROWS = 429
NB = 1162

MOMENTUM_RATE = 0.9
LEARN_RATE = 0.3
AVERAGE_RATE = 0.9

BF = jnp.bfloat16
F32 = jnp.float32
NN = (((1,), (0,)), ((), ()))
NT = (((1,), (1,)), ((), ()))
MESH = pl.DeviceIdType.MESH

E_ROWS = 640
I_BASE = EXPERTS * E_ROWS
I_ROWS = 864
GATE_AT = 416
TOWER_AT = 432
MISC_AT = 496
UPB_AT = 504
T_ROWS = 512


def split(v):
    hi = v.astype(BF)
    return hi, (v - hi.astype(F32)).astype(BF)


def dot(a, b, dims):
    return lax.dot_general(a, b, dims, preferred_element_type=F32)


def mm(a, b, dims=NN):
    return dot(a[0], b[0], dims) + (dot(a[1], b[0], dims) + dot(a[0], b[1], dims))


def sigmoid(v):
    return 1.0 / (1.0 + jnp.exp(-v))


def padded(rows, n):
    unit = 8 * n
    return (rows + unit - 1) // unit * unit


def step_kernel(
    n,
    chunks,
    total_rows,
    block,
    ids_hbm,
    len_hbm,
    dense_hbm,
    lab_hbm,
    tab_ref,
    inw_ref,
    upo_ref,
    dno_ref,
    upbo_ref,
    gate_ref,
    tw_ref,
    tout_ref,
    bias_ref,
    gexp_ref,
    grep_ref,
    ids_ref,
    len_ref,
    dense_ref,
    lab_ref,
    upx_ref,
    dnx_ref,
    upbx_ref,
    w_in,
    w_in_t,
    w_in_b,
    up_b,
    up_t,
    dn_b,
    dn_t,
    tw_b,
    gate_b,
    gate_t,
    cols,
    bcol,
    feat32,
    feat,
    x,
    h,
    bpd,
    bpu,
    dsu,
    mixed,
    bpt,
    bgl,
    thbl,
    bi,
    bp,
    sq,
    grads,
    r_core,
    r_one,
    r_two,
    r_z,
    in_sem,
    w_send,
    w_recv,
    s_sem,
    v_sem,
    zs_sem,
    zv_sem,
):
    dp = lax.axis_index("dp")
    hid = lax.axis_index("hid")
    nz = n // 4
    bx = dp % 2
    by = (dp // 2) % 2
    mz = dp // 4
    core_peer = (dp, 1 - hid)
    x_peer = (dp + 1 - 2 * bx, hid)
    y_peer = (dp + 2 - 4 * by, hid)
    z_peers = [((mz + k) % nz * 4 + dp % 4, hid) for k in range(1, nz)]

    rows = ids_ref.shape[2]
    lanes = pl.ds(pl.multiple_of(hid * rows, rows), rows)
    loads = [
        pltpu.make_async_copy(src, dst, in_sem.at[k])
        for k, (src, dst) in enumerate(
            (
                (ids_hbm.at[:, :, lanes], ids_ref),
                (len_hbm.at[:, lanes], len_ref),
                (dense_hbm.at[:, lanes], dense_ref),
                (lab_hbm.at[:, lanes], lab_ref),
            )
        )
    ]
    for load in loads:
        load.start()

    barrier = pltpu.get_barrier_semaphore()
    peers = [core_peer, x_peer, y_peer] + z_peers
    for peer in peers:
        pl.semaphore_signal(barrier, inc=1, device_id=peer, device_id_type=MESH)
    pl.semaphore_wait(barrier, len(peers))

    def remote(src, dst, send, recv, peer):
        return pltpu.make_async_remote_copy(
            src_ref=src, dst_ref=dst, send_sem=send, recv_sem=recv, device_id=peer, device_id_type=MESH
        )

    weights = [
        remote(src, dst, w_send.at[k], w_recv.at[k], core_peer)
        for k, (src, dst) in enumerate(((upo_ref, upx_ref), (dno_ref, dnx_ref), (upbo_ref, upbx_ref)))
    ]
    for copy in weights:
        copy.start()

    w_in[0:IN_ROWS, :] = inw_ref[...]
    row = lax.broadcasted_iota(jnp.int32, (8, D), 0)
    in_bias = jnp.broadcast_to(bias_ref[0:1, 0:D], (8, D))
    w_in[424:432, :] = jnp.where(row == 5, in_bias, jnp.where(row < 5, w_in[424:432, :], 0.0))
    w_in[432:512, :] = jnp.zeros((80, D), F32)
    for i in range(4):
        hi, lo = split(w_in[128 * i : 128 * (i + 1), :].T)
        w_in_t[0, :, 128 * i : 128 * (i + 1)] = hi
        w_in_t[1, :, 128 * i : 128 * (i + 1)] = lo
    hi, lo = split(w_in[0:POOLED, :])
    w_in_b[0] = hi
    w_in_b[1] = lo

    def expert_weights(k, up, down):
        for e in range(EXPERTS):
            c = 256 * e + 128 * k
            hi, lo = split(up[e])
            up_b[0, :, c : c + 128] = hi
            up_b[1, :, c : c + 128] = lo
            hi, lo = split(up[e].T)
            up_t[0, c : c + 128, :] = hi
            up_t[1, c : c + 128, :] = lo
            hi, lo = split(down[e])
            dn_b[0, c : c + 128, :] = hi
            dn_b[1, c : c + 128, :] = lo
            hi, lo = split(down[e].T)
            dn_t[0, e, :, 128 * k : 128 * k + 128] = hi
            dn_t[1, e, :, 128 * k : 128 * k + 128] = lo

    expert_weights(0, upo_ref, dno_ref)
    gate8 = jnp.concatenate([gate_ref[0], gate_ref[1]], 0)
    hi, lo = split(jnp.concatenate([gate8, jnp.zeros((8, D), F32)], 0))
    gate_b[0] = hi
    gate_b[1] = lo
    for i in range(4):
        tile = jnp.concatenate([gate8[:, 128 * i : 128 * (i + 1)], jnp.zeros((120, 128), F32)], 0).T
        hi, lo = split(tile)
        gate_t[0, 128 * i : 128 * (i + 1), :] = hi
        gate_t[1, 128 * i : 128 * (i + 1), :] = lo
    for t in range(TASKS):
        hi, lo = split(tw_ref[t])
        tw_b[0, TH * t : TH * t + TH, :] = hi
        tw_b[1, TH * t : TH * t + TH, :] = lo
    tw_t = split(jnp.concatenate([tw_ref[0], tw_ref[1]], 0).T)
    x[0, D : D + 16, :] = jnp.ones((16, rows), BF)
    x[1, D : D + 16, :] = jnp.zeros((16, rows), BF)
    sq[...] = jnp.zeros(sq.shape, F32)
    feat32[...] = jnp.zeros(feat32.shape, F32)

    for copy in weights:
        copy.wait()
    expert_weights(1, upx_ref, dnx_ref)
    biases = bias_ref[0:1, :]
    bcol[...] = jnp.zeros((128, 128), F32)
    bcol[0:4, :] = upbo_ref[...]
    bcol[4:8, :] = upbx_ref[...]
    for e in range(EXPERTS):
        bcol[8 + e : 9 + e, :] = biases[:, 512 + 128 * e : 640 + 128 * e]
    bcol[12:13, :] = biases[:, 1032:1160]
    bcol[13:14, 0:64] = tout_ref[0:1, :]
    bcol[13:14, 64:128] = tout_ref[1:2, :]
    bcol[14:15, 0:8] = biases[:, 1024:1032]
    cols[...] = bcol[...].T

    for load in loads:
        load.wait()

    scale = float(total_rows) ** -0.5

    def examples(i, carry):
        off = pl.multiple_of(i * block, block)
        here = pl.ds(off, block)

        def field(f, carry):
            lengths = len_ref[pl.ds(f, 1), here]
            table = [[tab_ref[f, 8 * a : 8 * a + 8, 128 * k : 128 * k + 128] for k in range(2)] for a in range(2)]
            for j in range(block // 128):
                length = jnp.broadcast_to(lengths[:, 128 * j : 128 * j + 128], (8, 128))
                sums = [jnp.zeros((8, 128), F32) for _ in range(2)]
                for s in range(4):
                    at = pl.ds(pl.multiple_of(off + 128 * j, 128), 128)
                    ident = jnp.broadcast_to(ids_ref[f, s : s + 1, at], (8, 128))
                    low = jnp.bitwise_and(ident, 127)
                    for a in range(2):
                        first = jnp.take_along_axis(table[a][0], low, axis=1, mode="promise_in_bounds")
                        second = jnp.take_along_axis(table[a][1], low, axis=1, mode="promise_in_bounds")
                        found = jnp.where(ident < 128, first, second)
                        sums[a] = sums[a] + jnp.where(length > s, found, 0.0)
                for a in range(2):
                    at = pl.ds(pl.multiple_of(16 * f + 8 * a, 8), 8)
                    feat32[at, 128 * j : 128 * j + 128] = sums[a]
            return carry

        lax.fori_loop(0, FIELDS, field, 0)
        feat32[POOLED:IN_ROWS, :] = dense_ref[:, here]
        feat32[IN_ROWS : IN_ROWS + 1, :] = jnp.ones((1, block), F32)
        fs = split(feat32[...])
        feat[0, :, here] = fs[0]
        feat[1, :, here] = fs[1]
        xv = mm((w_in_t[0], w_in_t[1]), fs)
        sq[0] += jnp.sum((xv * xv).reshape(D // 8, 8, block), axis=0)
        xs = split(xv)
        x[0, 0:D, here] = xs[0]
        x[1, 0:D, here] = xs[1]
        gate_logits = mm((gate_b[0], gate_b[1]), xs)[0:8] + cols[0:8, 14:15]
        gates = []
        for t in range(TASKS):
            r = [gate_logits[4 * t + e : 4 * t + e + 1] for e in range(EXPERTS)]
            top = jnp.maximum(jnp.maximum(r[0], r[1]), jnp.maximum(r[2], r[3]))
            ex = [jnp.exp(v - top) for v in r]
            inv = 1.0 / ((ex[0] + ex[1]) + (ex[2] + ex[3]))
            gates.append([v * inv for v in ex])
        outs = []
        slopes = []
        for e in range(EXPERTS):
            c = 256 * e
            pre = mm((up_t[0, c : c + 256, :], up_t[1, c : c + 256, :]), xs)
            pre = pre + jnp.concatenate([cols[:, e : e + 1], cols[:, 4 + e : 5 + e]], 0)
            s = sigmoid(pre)
            hv = pre * s
            dsu[c : c + 256, :] = s * (1.0 + pre * (1.0 - s))
            sq[1] += jnp.sum((hv * hv).reshape(HID // 8, 8, block), axis=0)
            hs = split(hv)
            h[0, c : c + 256, here] = hs[0]
            h[1, c : c + 256, here] = hs[1]
            pre = mm((dn_t[0, e], dn_t[1, e]), hs) + cols[:, 8 + e : 9 + e]
            s = sigmoid(pre)
            out = pre * s
            sq[2] += jnp.sum((out * out).reshape(OUT // 8, 8, block), axis=0)
            outs.append(out)
            slopes.append(s * (1.0 + pre * (1.0 - s)))
        back_mixed = []
        back_logit = []
        for t in range(TASKS):
            z = slice(TH * t, TH * t + TH)
            o = slice(OUT * t, OUT * t + OUT)
            g = gates[t]
            ms = split(g[0] * outs[0] + g[1] * outs[1] + g[2] * outs[2] + g[3] * outs[3])
            mixed[0, o, here] = ms[0]
            mixed[1, o, here] = ms[1]
            pre = mm((tw_b[0, z, :], tw_b[1, z, :]), ms) + cols[z, 12:13]
            s = sigmoid(pre)
            th = pre * s
            sq[3] += jnp.sum((th * th).reshape(TH // 8, 8, block), axis=0)
            wo = cols[z, 13:14]
            logit = jnp.sum(th * wo, axis=0, keepdims=True) + bias_ref[0:1, 1160 + t : 1161 + t]
            back = (sigmoid(logit) - lab_ref[t : t + 1, here].astype(F32)) * scale
            ths = split(th)
            thbl[0, z, here] = ths[0]
            thbl[1, z, here] = ths[1]
            bs = split(jnp.broadcast_to(back, (16, block)))
            thbl[0, 128 + 16 * t : 144 + 16 * t, here] = bs[0]
            thbl[1, 128 + 16 * t : 144 + 16 * t, here] = bs[1]
            bs = split(back * wo * (s * (1.0 + pre * (1.0 - s))))
            bpt[0, z, here] = bs[0]
            bpt[1, z, here] = bs[1]
            bm = mm((tw_t[0][:, z], tw_t[1][:, z]), bs)
            back_mixed.append(bm)
            bg = [jnp.sum(bm * outs[e], axis=0, keepdims=True) for e in range(EXPERTS)]
            mean = g[0] * bg[0] + g[1] * bg[1] + g[2] * bg[2] + g[3] * bg[3]
            back_logit += [g[e] * (bg[e] - mean) for e in range(EXPERTS)]
        bs = split(jnp.concatenate(back_logit + [jnp.zeros((8, block), F32)], 0))
        bgl[0, :, here] = bs[0]
        bgl[1, :, here] = bs[1]
        for e in range(EXPERTS):
            c = 256 * e
            bs = split((gates[0][e] * back_mixed[0] + gates[1][e] * back_mixed[1]) * slopes[e])
            bpd[0, OUT * e : OUT * e + OUT, here] = bs[0]
            bpd[1, OUT * e : OUT * e + OUT, here] = bs[1]
            bs = split(mm((dn_b[0, c : c + 256, :], dn_b[1, c : c + 256, :]), bs) * dsu[c : c + 256, :])
            bpu[0, c : c + 256, here] = bs[0]
            bpu[1, c : c + 256, here] = bs[1]
        return carry

    lax.fori_loop(0, rows // block, examples, 0)

    class Chunk:
        def __init__(self, c, base, size, expert):
            self.c, self.base, self.size, self.expert = c, base, size, expert
            one, two = ((bx, x_peer), (by, y_peer)) if c % 2 == 0 else ((by, y_peer), (bx, x_peer))
            self.b1, self.p1 = one
            self.b2, self.p2 = two
            self.o2 = base + self.b1 * (size // 2)
            self.o3 = self.o2 + self.b2 * (size // 4)
            self.piece = size // 4 // nz
            self.o4 = self.o3 + mz * self.piece

        def at(self, start, size):
            return pl.ds(pl.multiple_of(start, 8), size)

        def res(self, start, size):
            if self.expert:
                return gexp_ref.at[self.at(start, size)]
            return grep_ref.at[hid, self.at(start - I_PAD, size)]

        def sems(self, k):
            return s_sem.at[8 * self.c + k], v_sem.at[8 * self.c + k]

        def core_start(self):
            rng = self.at(self.base, self.size)
            self.core = remote(grads.at[1, rng], r_core.at[rng], *self.sems(0), core_peer)
            self.core.start()

        def one_start(self):
            self.core.wait()
            rng = self.at(self.base, self.size)
            grads[0, rng, :] += r_core[rng, :]
            half = self.size // 2
            src = self.at(self.base + (1 - self.b1) * half, half)
            self.one = remote(
                grads.at[0, src], r_one.at[self.at(self.base // 2, half)], *self.sems(1), self.p1
            )
            self.one.start()

        def two_start(self):
            self.one.wait()
            half = self.size // 2
            grads[0, self.at(self.o2, half), :] += r_one[self.at(self.base // 2, half), :]
            quarter = self.size // 4
            src = self.at(self.o2 + (1 - self.b2) * quarter, quarter)
            self.two = remote(
                grads.at[0, src], r_two.at[self.at(self.base // 4, quarter)], *self.sems(2), self.p2
            )
            self.two.start()

        def z_start(self):
            self.two.wait()
            quarter = self.size // 4
            grads[0, self.at(self.o3, quarter), :] += r_two[self.at(self.base // 4, quarter), :]
            self.z = []
            for k in range(1, nz):
                src = self.at(self.o3 + (mz + k) % nz * self.piece, self.piece)
                dst = r_z.at[nz - k - 1, self.at(self.base // (4 * nz), self.piece)]
                q = self.c * (nz - 1)
                self.z.append(
                    remote(
                        grads.at[0, src], dst, zs_sem.at[0, q + k - 1], zv_sem.at[0, q + nz - k - 1], z_peers[k - 1]
                    )
                )
            for copy in self.z:
                copy.start()

        def z_gather(self):
            for copy in self.z:
                copy.wait()
            mine = self.at(self.o4, self.piece)
            total = grads[0, mine, :]
            for k in range(nz - 1):
                total = total + r_z[k, self.at(self.base // (4 * nz), self.piece), :]
            out = self.res(self.o4, self.piece)
            out[...] = total
            self.z = []
            for k in range(1, nz):
                q = self.c * (nz - 1)
                self.z.append(
                    remote(out, out, zs_sem.at[1, q + k - 1], zv_sem.at[1, q + nz - k - 1], z_peers[k - 1])
                )
            for copy in self.z:
                copy.start()

        def two_gather(self):
            for copy in self.z:
                copy.wait()
            out = self.res(self.o3, self.size // 4)
            self.two = remote(out, out, *self.sems(3), self.p2)
            self.two.start()

        def one_gather(self):
            self.two.wait()
            out = self.res(self.o2, self.size // 2)
            self.one = remote(out, out, *self.sems(4), self.p1)
            self.one.start()

        def core_gather(self):
            self.one.wait()
            if not self.expert:
                out = self.res(self.base, self.size)
                self.core = remote(out, out, *self.sems(5), core_peer)
                self.core.start()

        def finish(self):
            if not self.expert:
                self.core.wait()

    I_PAD = chunks[EXPERTS][0]
    parts = [Chunk(c, base, size, c < EXPERTS) for c, (base, size) in enumerate(chunks)]

    t_base, t_size = chunks[EXPERTS + 1]
    misc = t_base + MISC_AT
    grads[:, misc : t_base + t_size, :] = jnp.zeros((2, t_size - MISC_AT, 128), F32)
    for e in range(EXPERTS):
        c, o = 256 * e, 128 * e
        base = chunks[e][0]
        g = mm((x[0], x[1]), (bpu[0, c : c + 256, :], bpu[1, c : c + 256, :]), NT)
        grads[0, base : base + D, :] = g[0:D, 0:128]
        grads[1, base : base + D, :] = g[0:D, 128:256]
        upb = chunks[5][0] + UPB_AT + e
        grads[0, upb : upb + 1, :] = g[D : D + 1, 0:128]
        grads[1, upb : upb + 1, :] = g[D : D + 1, 128:256]
        g = mm((h[0, c : c + 256, :], h[1, c : c + 256, :]), (bpd[0, o : o + 128, :], bpd[1, o : o + 128, :]), NT)
        grads[0, base + D : base + E_ROWS, :] = g[0:128]
        grads[1, base + D : base + E_ROWS, :] = g[128:256]
        if chunks[e][1] > E_ROWS:
            grads[:, base + E_ROWS : base + chunks[e][1], :] = jnp.zeros((2, chunks[e][1] - E_ROWS, 128), F32)
        parts[e].core_start()

    def inputs_back(i, carry):
        here = pl.ds(pl.multiple_of(i * block, block), block)
        b = mm((up_b[0], up_b[1]), (bpu[0, :, here], bpu[1, :, here]))
        b = b + mm((gate_t[0, :, 0:16], gate_t[1, :, 0:16]), (bgl[0, :, here], bgl[1, :, here]))
        bs = split(b)
        bi[0, :, here] = bs[0]
        bi[1, :, here] = bs[1]
        ps = split(mm((w_in_b[0], w_in_b[1]), bs))
        bp[0, :, here] = ps[0]
        bp[1, :, here] = ps[1]
        return carry

    lax.fori_loop(0, rows // block, inputs_back, 0)

    def owner(k):
        return (k + hid) % 2

    i_base, i_size = chunks[EXPERTS]
    for k in range(4):
        g = mm((feat[0], feat[1]), (bi[0, 128 * k : 128 * k + 128, :], bi[1, 128 * k : 128 * k + 128, :]), NT)
        at = i_base + 432 * (k % 2)
        grads[owner(k // 2), at : at + 432, :] = g[0:432]
    if i_size > I_ROWS:
        grads[:, i_base + I_ROWS : i_base + i_size, :] = jnp.zeros((2, i_size - I_ROWS, 128), F32)
    parts[4].core_start()

    one16 = jnp.ones((16, rows), BF)
    g = mm((bgl[0], bgl[1]), (x[0], x[1]), NT)
    for k in range(4):
        at = t_base + GATE_AT + 8 * (k % 2)
        grads[owner(k // 2), at : at + 8, :] = g[0:8, 128 * k : 128 * k + 128]
    for t in range(TASKS):
        z = slice(TH * t, TH * t + TH)
        o = slice(OUT * t, OUT * t + OUT)
        g = mm((bpt[0, z, :], bpt[1, z, :]), (mixed[0, o, :], mixed[1, o, :]), NT)
        grads[owner(t), t_base + TOWER_AT : t_base + TOWER_AT + TH, :] = g
    lane = lax.broadcasted_iota(jnp.int32, (1, 128), 1)
    g = dot(one16, bpd[0], NT) + dot(one16, bpd[1], NT)
    m = owner(0)
    for e in range(EXPERTS):
        grads[m, misc + e : misc + e + 1, :] = g[0:1, 128 * e : 128 * e + 128]
    g = dot(one16, bpt[0], NT) + dot(one16, bpt[1], NT)
    grads[m, misc + 4 : misc + 5, :] = g[0:1]
    g = mm((thbl[0, 128:160, :], thbl[1, 128:160, :]), (thbl[0, 0:128, :], thbl[1, 0:128, :]), NT)
    grads[m, misc + 5 : misc + 6, :] = jnp.where(lane < TH, g[0:1], g[16:17])
    g = dot(one16, bgl[0], NT) + dot(one16, bgl[1], NT)
    grads[m, misc + 6 : misc + 7, 0:8] = g[0:1, 0:8]
    g = dot(one16, thbl[0, 128:160, :], NT) + dot(one16, thbl[1, 128:160, :], NT)
    grads[m, misc + 6 : misc + 7, 8:9] = g[0:1, 0:1]
    grads[m, misc + 6 : misc + 7, 9:10] = g[0:1, 16:17]
    sums = jnp.sum(sq[...], axis=(1, 2), keepdims=True).reshape(4, 1)
    squares = jnp.zeros((1, 128), F32)
    for k in range(4):
        squares = jnp.where(lane == k, sums[k : k + 1, :], squares)
    grads[m, misc + 7 : misc + 8, :] = squares

    def table_field(f, carry):
        lengths = len_ref[pl.ds(f, 1), :]
        ident = [jnp.where(lengths > s, ids_ref[f, s : s + 1, :], 512).astype(F32).astype(BF) for s in range(4)]
        at = pl.ds(pl.multiple_of(EMB * f, EMB), EMB)
        total = jnp.zeros((2 * EMB, VOCAB), F32)
        vocab = lax.broadcasted_iota(jnp.int32, (VOCAB, block), 0).astype(F32).astype(BF)
        one, zero = jnp.ones((VOCAB, block), BF), jnp.zeros((VOCAB, block), BF)
        for j in range(rows // block):
            here = slice(block * j, block * (j + 1))
            counts = zero
            for s in range(4):
                counts = counts + jnp.where(jnp.broadcast_to(ident[s][:, here], (VOCAB, block)) == vocab, one, zero)
            total = total + dot(jnp.concatenate([bp[0, at, here], bp[1, at, here]], 0), counts, NT)
        g = total[0:EMB] + total[EMB : 2 * EMB]
        at = pl.ds(pl.multiple_of(t_base + EMB * f, EMB), EMB)
        grads[owner(0), at, :] = g[:, 0:128]
        grads[owner(1), at, :] = g[:, 128:256]
        return carry

    lax.fori_loop(0, FIELDS, table_field, 0)
    parts[5].core_start()

    for stage in ("one_start", "two_start", "z_start", "z_gather", "two_gather", "one_gather", "core_gather", "finish"):
        for part in parts:
            getattr(part, stage)()


def step(ids, lengths, dense, labels, tables, in_weight, up, down, up_bias, gate, tower, tower_out, biases, n, total_rows):
    rows = ids.shape[2] // 2
    block = 256
    sizes = [padded(E_ROWS, n)] * EXPERTS + [padded(I_ROWS, n), padded(T_ROWS, n)]
    chunks = []
    base = 0
    for size in sizes:
        chunks.append((base, size))
        base += size
    e_all = chunks[EXPERTS][0]
    nz = n // 4
    vm = pltpu.VMEM
    scratch = [
        vm((FIELDS, 4, rows), jnp.int32),
        vm((FIELDS, rows), jnp.int32),
        vm((13, rows), F32),
        vm((TASKS, rows), jnp.int32),
        vm((EXPERTS, D, 128), F32),
        vm((EXPERTS, 128, OUT), F32),
        vm((EXPERTS, 128), F32),
        vm((512, D), F32),
        vm((2, D, 512), BF),
        vm((2, POOLED, D), BF),
        vm((2, D, EXPERTS * HID), BF),
        vm((2, EXPERTS * HID, D), BF),
        vm((2, EXPERTS * HID, OUT), BF),
        vm((2, EXPERTS, OUT, HID), BF),
        vm((2, TASKS * TH, OUT), BF),
        vm((2, 16, D), BF),
        vm((2, D, 128), BF),
        vm((128, 128), F32),
        vm((128, 128), F32),
        vm((512, block), F32),
        vm((2, 512, rows), BF),
        vm((2, D + 16, rows), BF),
        vm((2, EXPERTS * HID, rows), BF),
        vm((2, EXPERTS * OUT, rows), BF),
        vm((2, EXPERTS * HID, rows), BF),
        vm((EXPERTS * HID, block), F32),
        vm((2, TASKS * OUT, rows), BF),
        vm((2, TASKS * TH, rows), BF),
        vm((2, 16, rows), BF),
        vm((2, 160, rows), BF),
        vm((2, D, rows), BF),
        vm((2, POOLED, rows), BF),
        vm((4, 8, block), F32),
        vm((2, base, 128), F32),
        vm((base, 128), F32),
        vm((base // 2, 128), F32),
        vm((base // 4, 128), F32),
        vm((nz - 1, base // n, 128), F32),
        pltpu.SemaphoreType.DMA((4,)),
        pltpu.SemaphoreType.DMA((3,)),
        pltpu.SemaphoreType.DMA((3,)),
        pltpu.SemaphoreType.DMA((8 * len(chunks),)),
        pltpu.SemaphoreType.DMA((8 * len(chunks),)),
        pltpu.SemaphoreType.DMA((2, len(chunks) * (nz - 1))),
        pltpu.SemaphoreType.DMA((2, len(chunks) * (nz - 1))),
    ]
    anywhere = pl.BlockSpec(memory_space=pl.ANY)
    local = pl.BlockSpec(memory_space=pltpu.VMEM)
    return pl.pallas_call(
        functools.partial(step_kernel, n, chunks, total_rows, block),
        out_shape=[
            jax.ShapeDtypeStruct((e_all, 128), F32),
            jax.ShapeDtypeStruct((2, base - e_all, 128), F32),
        ],
        in_specs=[anywhere] * 4 + [local] * 9,
        out_specs=[local] * 2,
        scratch_shapes=scratch,
        compiler_params=pltpu.CompilerParams(collective_id=0, has_side_effects=True, vmem_limit_bytes=62 << 20),
        name="step",
    )(ids, lengths, dense, labels, tables, in_weight, up, down, up_bias, gate, tower, tower_out, biases)


def update_kernel(e_size, i_size, counts, gexp_ref, grep_ref, *refs):
    hid = lax.axis_index("hid")
    params = [refs[3 * k : 3 * k + 3] for k in range(9)]
    results = [refs[27 + 4 * k : 31 + 4 * k] for k in range(9)]
    rms_ref = refs[63]

    def update(k, at, g):
        w_ref, m_ref, a_ref = params[k]
        new_m = MOMENTUM_RATE * m_ref[at] + g
        new_w = w_ref[at] - LEARN_RATE * (g + MOMENTUM_RATE * new_m)
        ow, om, oa, orr = results[k]
        ow[at] = new_w
        om[at] = new_m
        oa[at] = AVERAGE_RATE * a_ref[at] + (1.0 - AVERAGE_RATE) * new_w
        orr[at] = new_w.astype(BF)

    t = i_size
    everything = slice(None)
    for f in range(FIELDS):
        for k in range(2):
            update(0, (f, everything, slice(128 * k, 128 * k + 128)), grep_ref[k, t + EMB * f : t + EMB * f + EMB, :])
    for k in range(4):
        at = 432 * (k % 2)
        update(1, (everything, slice(128 * k, 128 * k + 128)), grep_ref[k // 2, at : at + IN_ROWS, :])
    for e in range(EXPERTS):
        at = e_size * e
        update(2, (e,), gexp_ref[at : at + D, :])
        update(3, (e,), gexp_ref[at + D : at + E_ROWS, :])
    update(4, (everything,), grep_ref[hid, t + UPB_AT : t + UPB_AT + 4, :])
    for k in range(4):
        at = t + GATE_AT + 8 * (k % 2)
        for s in range(TASKS):
            g = grep_ref[k // 2, at + 4 * s : at + 4 * s + 4, :]
            update(5, (s, everything, slice(128 * k, 128 * k + 128)), g)
    for s in range(TASKS):
        update(6, (s,), grep_ref[s, t + TOWER_AT : t + TOWER_AT + TH, :])
    misc = t + MISC_AT
    tout = grep_ref[0, misc + 5 : misc + 6, :]
    for s in range(TASKS):
        update(7, (slice(s, s + 1), everything), tout[:, TH * s : TH * s + TH])
    pieces = [grep_ref[k // 2, 432 * (k % 2) + IN_ROWS : 432 * (k % 2) + IN_ROWS + 1, :] for k in range(4)]
    pieces += [grep_ref[0, misc + e : misc + e + 1, :] for e in range(EXPERTS)]
    last = grep_ref[0, misc + 6 : misc + 7, :]
    pieces += [last[:, 0:8], grep_ref[0, misc + 4 : misc + 5, :], last[:, 8:10]]
    update(8, (everything,), jnp.concatenate(pieces, 1))
    squares = grep_ref[0, misc + 7 : misc + 8, 0:4]
    lane = lax.broadcasted_iota(jnp.int32, (1, 4), 1)
    inverse = jnp.zeros((1, 4), F32)
    for k, count in enumerate(counts):
        inverse = jnp.where(lane == k, 1.0 / count, inverse)
    rms_ref[...] = jnp.sqrt(squares * inverse + 1e-06)


def local(*args):
    n = lax.axis_size("dp")
    ids, lengths, dense, labels = args[:4]
    total_rows = ids.shape[0] * n
    params = [list(args[4 + 3 * k : 7 + 3 * k]) for k in range(9)]
    for k in (0, 5, 6):
        params[k] = [v.transpose(0, 2, 1) for v in params[k]]
    params[8] = [v.reshape(1, NB) for v in params[8]]
    gexp, grep = step(
        ids.transpose(1, 2, 0),
        lengths.T,
        dense.T,
        labels.T,
        *[p[0] for p in params],
        n=n,
        total_rows=total_rows,
    )
    counts = [float(total_rows * c) for c in (D, EXPERTS * HID, EXPERTS * OUT, TASKS * TH)]
    shapes = []
    for p in params:
        shapes += [jax.ShapeDtypeStruct(p[0].shape, F32)] * 3 + [jax.ShapeDtypeStruct(p[0].shape, BF)]
    shapes.append(jax.ShapeDtypeStruct((1, 4), F32))
    flat = [v for p in params for v in p]
    vmem = pl.BlockSpec(memory_space=pltpu.VMEM)
    outs = pl.pallas_call(
        functools.partial(update_kernel, padded(E_ROWS, n), padded(I_ROWS, n), counts),
        out_shape=shapes,
        in_specs=[vmem] * (2 + len(flat)),
        out_specs=[vmem] * len(shapes),
        compiler_params=pltpu.CompilerParams(vmem_limit_bytes=62 << 20),
        name="update",
    )(gexp, grep, *flat)
    outs = list(outs)
    for k in (0, 5, 6):
        outs[4 * k : 4 * k + 4] = [v.transpose(0, 2, 1) for v in outs[4 * k : 4 * k + 4]]
    outs[32:36] = [v.reshape(NB) for v in outs[32:36]]
    outs[36] = outs[36].reshape(4)
    return tuple(outs)


def solution(mesh):
    up, down, bias = P(None, None, "hid"), P(None, "hid", None), P(None, "hid")
    rep = P()
    return jax.shard_map(
        local,
        mesh=mesh,
        in_specs=(P("dp", None, None), P("dp", None), P("dp", None), P("dp", None))
        + (rep,) * 6
        + (up,) * 3
        + (down,) * 3
        + (bias,) * 3
        + (rep,) * 12,
        out_specs=(rep,) * 8 + (up,) * 4 + (down,) * 4 + (bias,) * 4 + (rep,) * 17,
        check_vma=False,
    )
```

profile of v0, /device:TPU:0, one launch (start us, length us, event | category | flops | bytes accessed | tf_op | source)
XLA Modules:
  0.0 153.7 jit_solution(13748481813309399012)
XLA Ops:
  0.7 1.3 reshape.98.bias_ref.refs_24_
  2.0 1.3 reshape.99.refs_25_
  3.3 1.3 reshape.100.refs_26_
  4.6 135.7 %step.1 = (f32[2560,128]{1,0:T(8,128)}, f32[2,1408,128]{2,1,0:T(8,128)}) custom-call(s32[26,4,2048]{2,1,0:T(4,128)} %bitcast.28, s32[26,2048]{1,0:T(8,128)} %bitcast.33, f32[13,2048]{1,0:T(8,128)} %bitcast.34, s32[2,2048]{1,0:T(2,128)} %bitcast.39, f32[26,16,256]{2,1,0:T(8,128)} %bitcast.26, f32[429,512]{1,0:T(8,128)} %refs_3_.1, f32[4,512,128]{2,1,0:T(8,128)} %refs_6_.1, ...), custom_call_target="tpu_custom_call" | custom-call | tf_op jit(solution)/shard_map/step/pallas_call | solution.py:626
  140.3 8.1 %update.1 = (f32[26,16,256]{2,1,0:T(8,128)}, f32[26,16,256]{2,1,0:T(8,128)}, f32[26,16,256]{2,1,0:T(8,128)}, bf16[26,16,256]{2,1,0:T(8,128)(2,1)}, f32[429,512]{...) custom-call(f32[2560,128]{1,0:T(8,128)} %get-tuple-element.76.gexp_r, ...), custom_call_target="tpu_custom_call" | custom-call | tf_op jit(solution)/shard_map/update/pallas_call | solution.py:717
  148.4 1.3 reduce.3
  149.7 1.3 reduce
  151.0 1.3 reduce.1
  152.3 1.3 reduce.2
where the time goes:
time: 154 us
  Pallas kernels  144 us (94%)
  other arithmetic  5.22 us (3%)
  local copies, waits for them, and re-layouts  3.88 us (3%)
    pallas_call x1, Pallas kernels, step(): pl.pallas_call(functools.partial(step_kernel, n, chunks, total_rows, bloc...  136 us
    pallas_call x1, Pallas kernels, local(): pl.pallas_call(functools.partial(update_kernel, padded(E_ROWS, n), padded...  8.12 us
    pallas_call x4, other arithmetic, local(): pl.pallas_call(functools.partial(update_kernel, padded(E_ROWS, n), padded...  5.22 us
    reshape x3, local copies, waits for them, and re-layouts, local(): params[8] = [v.reshape(1, NB) for v in params[8]]  3.88 us

commit v1 on v0

v1 whole, which is shorter than its diff:
```python
import functools

import jax
import jax.numpy as jnp
from jax import lax
from jax.experimental import pallas as pl
from jax.experimental.pallas import tpu as pltpu
from jax.sharding import PartitionSpec as P

D = 512
HID = 256
OUT = 128
TH = 64
TASKS = 2
EXPERTS = 4
FIELDS = 26
VOCAB = 256
EMB = 16
POOLED = 416
IN_ROWS = 429
NB = 1162

MOMENTUM_RATE = 0.9
LEARN_RATE = 0.3
AVERAGE_RATE = 0.9

BF = jnp.bfloat16
F32 = jnp.float32
NN = (((1,), (0,)), ((), ()))
NT = (((1,), (1,)), ((), ()))
MESH = pl.DeviceIdType.MESH

E_ROWS = 640
I_BASE = EXPERTS * E_ROWS
I_ROWS = 864
GATE_AT = 416
TOWER_AT = 432
MISC_AT = 496
UPB_AT = 504
T_ROWS = 512


def split(v):
    hi = v.astype(BF)
    return hi, (v - hi.astype(F32)).astype(BF)


def dot(a, b, dims):
    return lax.dot_general(a, b, dims, preferred_element_type=F32)


def mm(a, b, dims=NN):
    return dot(a[0], b[0], dims) + (dot(a[1], b[0], dims) + dot(a[0], b[1], dims))


def bag_counts(part_ref, f, here, width):
    row = lax.broadcasted_iota(jnp.int32, (16, width), 0).astype(F32).astype(BF)
    zero = jnp.zeros((16, width), BF)
    weights = [jnp.broadcast_to(part_ref[0, f, s : s + 1, here], (16, width)).astype(BF) for s in range(4)]
    offsets = [jnp.broadcast_to(part_ref[1, f, s : s + 1, here], (16, width)).astype(BF) - row for s in range(4)]
    low, high = [], []
    for t in range(8):
        start = jnp.full((16, width), 16 * t, BF)
        hit = [jnp.where(offsets[s] == start, weights[s], zero) for s in range(4)]
        both = (hit[0] + hit[1]) + (hit[2] + hit[3])
        whole = (both + 128.0) - 128.0
        low.append(both - whole)
        high.append(whole)
    return jnp.concatenate(low + high, 0)


def step_kernel(
    n,
    chunks,
    total_rows,
    ids_hbm,
    len_hbm,
    dense_hbm,
    lab_hbm,
    tab_hbm,
    inw_hbm,
    up_hbm,
    dn_hbm,
    upbo_ref,
    gate_ref,
    tw_ref,
    tout_ref,
    bias_ref,
    gexp_ref,
    grep_ref,
    ids_ref,
    len_ref,
    dense_ref,
    lab_ref,
    tab_ref,
    up_ref,
    dn_ref,
    upbx_ref,
    brow,
    part,
    w_raw,
    w_in,
    w_in_t,
    w_in_b,
    up_b,
    up_t,
    dn_b,
    dn_t,
    tw_b,
    gate_t,
    cols,
    bcol,
    feat,
    x,
    h,
    bpd,
    bpu,
    dsu,
    mixed,
    bpt,
    bgl,
    thbl,
    bi,
    bp,
    grads,
    r_core,
    r_one,
    r_two,
    r_z,
    in_sem,
    w_send,
    w_recv,
    s_sem,
    v_sem,
    zs_sem,
    zv_sem,
):
    dp = lax.axis_index("dp")
    hid = lax.axis_index("hid")
    nz = n // 4
    bx = dp % 2
    by = (dp // 2) % 2
    mz = dp // 4
    core_peer = (dp, 1 - hid)
    x_peer = (dp + 1 - 2 * bx, hid)
    y_peer = (dp + 2 - 4 * by, hid)
    z_peers = [((mz + k) % nz * 4 + dp % 4, hid) for k in range(1, nz)]

    barrier = pltpu.get_barrier_semaphore()
    peers = [core_peer, x_peer, y_peer] + z_peers
    for peer in peers:
        pl.semaphore_signal(barrier, inc=1, device_id=peer, device_id_type=MESH)

    rows = ids_ref.shape[2]
    lanes = pl.ds(pl.multiple_of(hid * rows, rows), rows)
    loads = [
        pltpu.make_async_copy(src, dst, in_sem.at[k])
        for k, (src, dst) in enumerate(
            (
                (ids_hbm.at[:, :, lanes], ids_ref),
                (len_hbm.at[:, lanes], len_ref),
                (tab_hbm, tab_ref),
                (inw_hbm, w_raw),
                (up_hbm, up_ref.at[0]),
                (dn_hbm, dn_ref.at[0]),
                (dense_hbm.at[:, lanes], dense_ref),
                (lab_hbm.at[:, lanes], lab_ref),
            )
        )
    ]
    for load in loads:
        load.start()

    def remote(src, dst, send, recv, peer):
        return pltpu.make_async_remote_copy(
            src_ref=src, dst_ref=dst, send_sem=send, recv_sem=recv, device_id=peer, device_id_type=MESH
        )

    loads[0].wait()
    loads[1].wait()
    slot = lax.broadcasted_iota(jnp.int32, (4, rows), 0)
    for f in range(FIELDS):
        used = jnp.broadcast_to(len_ref[f : f + 1, :], (4, rows)) > slot
        ident = ids_ref[f]
        part[0, f] = jnp.where(used, jnp.where(ident < 128, 0.0625, 1.0), 0.0)
        part[1, f] = jnp.bitwise_and(ident, 127).astype(F32)

    pl.semaphore_wait(barrier, len(peers))
    weights = [
        remote(src, dst, w_send.at[k], w_recv.at[k], core_peer)
        for k, (src, dst) in enumerate(((up_hbm, up_ref.at[1]), (dn_hbm, dn_ref.at[1]), (upbo_ref, upbx_ref)))
    ]
    for copy in weights:
        copy.start()

    loads[2].wait()
    sixteen = jnp.where(lax.broadcasted_iota(jnp.int32, (EMB, VOCAB), 1) < 128, 16.0, 1.0)
    width = 256

    def pool_fields(i, carry):
        for u in range(2):
            f = 2 * i + u
            table = jnp.concatenate(split(tab_ref[f] * sixteen), 0)
            at = pl.ds(pl.multiple_of(EMB * f, EMB), EMB)
            for j in range(rows // width):
                here = slice(width * j, width * (j + 1))
                both = dot(table, bag_counts(part, f, here, width), NN)
                hi, lo = split(both[0:EMB] + both[EMB : 2 * EMB])
                feat[0, at, here] = hi
                feat[1, at, here] = lo
        return carry

    lax.fori_loop(0, FIELDS // 2, pool_fields, 0)

    brow[0:1, 0:1024] = bias_ref[0:1024].reshape(1, 1024)
    brow[0:1, 1024:NB] = bias_ref[1024:NB].reshape(1, NB - 1024)
    biases = brow[0:1, 0:NB]
    loads[3].wait()
    row = lax.broadcasted_iota(jnp.int32, (8, D), 0)
    in_bias = jnp.broadcast_to(biases[:, 0:D], (8, D))
    w_in[0:IN_ROWS, :] = w_raw[...]
    w_in[424:432, :] = jnp.where(row == 5, in_bias, jnp.where(row < 5, w_in[424:432, :], 0.0))
    w_in[432:512, :] = jnp.zeros((80, D), F32)
    for i in range(4):
        hi, lo = split(w_in[128 * i : 128 * (i + 1), :].T)
        w_in_t[0, :, 128 * i : 128 * (i + 1)] = hi
        w_in_t[1, :, 128 * i : 128 * (i + 1)] = lo
    hi, lo = split(w_in[0:POOLED, :])
    w_in_b[0] = hi
    w_in_b[1] = lo

    def expert_weights(k):
        for e in range(EXPERTS):
            c = 256 * e + 128 * k
            up, down = up_ref[k, e], dn_ref[k, e]
            hi, lo = split(up)
            up_b[0, :, c : c + 128] = hi
            up_b[1, :, c : c + 128] = lo
            hi, lo = split(up.T)
            up_t[0, c : c + 128, :] = hi
            up_t[1, c : c + 128, :] = lo
            hi, lo = split(down)
            dn_b[c : c + 128, 0:128] = hi
            dn_b[c : c + 128, 128:256] = lo
            hi, lo = split(down.T)
            dn_t[0, e, :, 128 * k : 128 * k + 128] = hi
            dn_t[1, e, :, 128 * k : 128 * k + 128] = lo

    loads[4].wait()
    loads[5].wait()
    expert_weights(0)
    gate8 = jnp.concatenate([gate_ref[0], gate_ref[1]], 0)
    hi, lo = split(jnp.concatenate([gate8, jnp.zeros((8, D), F32)], 0))
    up_t[0, 1024:1040, :] = hi
    up_t[1, 1024:1040, :] = lo
    for i in range(4):
        tile = jnp.concatenate([gate8[:, 128 * i : 128 * (i + 1)], jnp.zeros((120, 128), F32)], 0).T
        hi, lo = split(tile)
        gate_t[0, 128 * i : 128 * (i + 1), :] = hi
        gate_t[1, 128 * i : 128 * (i + 1), :] = lo
    for t in range(TASKS):
        hi, lo = split(tw_ref[t])
        tw_b[TH * t : TH * t + TH, 0:128] = hi
        tw_b[TH * t : TH * t + TH, 128:256] = lo
    tw_t = split(jnp.concatenate([tw_ref[0], tw_ref[1]], 0).T)
    x[0, D : D + 16, :] = jnp.ones((16, rows), BF)
    x[1, D : D + 16, :] = jnp.zeros((16, rows), BF)
    loads[6].wait()
    loads[7].wait()
    hi, lo = split(jnp.concatenate([dense_ref[...], jnp.ones((1, rows), F32), jnp.zeros((2, rows), F32)], 0))
    feat[0, POOLED:432, :] = hi
    feat[1, POOLED:432, :] = lo

    for copy in weights:
        copy.wait()
    expert_weights(1)
    bcol[...] = jnp.zeros((128, 128), F32)
    bcol[0:4, :] = upbo_ref[...]
    bcol[4:8, :] = upbx_ref[...]
    for e in range(EXPERTS):
        bcol[8 + e : 9 + e, :] = biases[:, 512 + 128 * e : 640 + 128 * e]
    bcol[12:13, :] = biases[:, 1032:1160]
    bcol[13:14, 0:64] = tout_ref[0:1, :]
    bcol[13:14, 64:128] = tout_ref[1:2, :]
    bcol[14:15, 0:8] = biases[:, 1024:1032]
    cols[...] = bcol[...].T

    scale = float(total_rows) ** -0.5
    fs = (feat[0], feat[1])
    xv = mm((w_in_t[0, :, 0:432], w_in_t[1, :, 0:432]), fs)
    squares = [jnp.sum(xv * xv, keepdims=True)]
    xs = split(xv)
    x[0, 0:D, :] = xs[0]
    x[1, 0:D, :] = xs[1]
    gate_logits = mm((up_t[0, 1024:1040], up_t[1, 1024:1040]), xs)[0:8] + cols[0:8, 14:15]
    gates = []
    for t in range(TASKS):
        r = [gate_logits[4 * t + e : 4 * t + e + 1] for e in range(EXPERTS)]
        top = jnp.maximum(jnp.maximum(r[0], r[1]), jnp.maximum(r[2], r[3]))
        ex = [jnp.exp(v - top) for v in r]
        inv = 1.0 / ((ex[0] + ex[1]) + (ex[2] + ex[3]))
        gates.append([v * inv for v in ex])
    outs, slopes = [], []
    sums = [0.0, 0.0, 0.0]
    for e in range(EXPERTS):
        c = 256 * e
        pre = mm((up_t[0, c : c + 256, :], up_t[1, c : c + 256, :]), xs)
        pre = pre + jnp.concatenate([cols[:, e : e + 1], cols[:, 4 + e : 5 + e]], 0)
        s = jax.nn.sigmoid(pre)
        hv = pre * s
        dsu[c : c + 256, :] = s + hv * (1.0 - s)
        sums[0] = sums[0] + jnp.sum(hv * hv, keepdims=True)
        hs = split(hv)
        h[0, c : c + 256, :] = hs[0]
        h[1, c : c + 256, :] = hs[1]
        pre = mm((dn_t[0, e], dn_t[1, e]), hs) + cols[:, 8 + e : 9 + e]
        s = jax.nn.sigmoid(pre)
        out = pre * s
        sums[1] = sums[1] + jnp.sum(out * out, keepdims=True)
        outs.append(out)
        slopes.append(s + out * (1.0 - s))
    back_mixed, back_logit = [], []
    for t in range(TASKS):
        z = slice(TH * t, TH * t + TH)
        o = slice(OUT * t, OUT * t + OUT)
        g = gates[t]
        ms = split(g[0] * outs[0] + g[1] * outs[1] + g[2] * outs[2] + g[3] * outs[3])
        mixed[0, o, :] = ms[0]
        mixed[1, o, :] = ms[1]
        w = tw_b[z, :]
        pre = dot(w, jnp.concatenate([ms[0], ms[0]], 0), NN) + dot(w[:, 0:128], ms[1], NN) + cols[z, 12:13]
        s = jax.nn.sigmoid(pre)
        th = pre * s
        sums[2] = sums[2] + jnp.sum(th * th, keepdims=True)
        wo = cols[z, 13:14]
        logit = jnp.sum(th * wo, axis=0, keepdims=True) + biases[:, 1160 + t : 1161 + t]
        back = (jax.nn.sigmoid(logit) - lab_ref[t : t + 1, :].astype(F32)) * scale
        ths = split(th)
        thbl[0, z, :] = ths[0]
        thbl[1, z, :] = ths[1]
        bs = split(jnp.broadcast_to(back, (16, rows)))
        thbl[0, 128 + 16 * t : 144 + 16 * t, :] = bs[0]
        thbl[1, 128 + 16 * t : 144 + 16 * t, :] = bs[1]
        bs = split(back * wo * (s + th * (1.0 - s)))
        bpt[0, z, :] = bs[0]
        bpt[1, z, :] = bs[1]
        w = [v[:, z] for v in tw_t]
        bm = dot(jnp.concatenate([w[0], w[1], w[0]], 1), jnp.concatenate([bs[0], bs[0], bs[1]], 0), NN)
        back_mixed.append(bm)
        bg = [jnp.sum(bm * outs[e], axis=0, keepdims=True) for e in range(EXPERTS)]
        mean = g[0] * bg[0] + g[1] * bg[1] + g[2] * bg[2] + g[3] * bg[3]
        back_logit += [g[e] * (bg[e] - mean) for e in range(EXPERTS)]
    bs = split(jnp.concatenate(back_logit + [jnp.zeros((8, rows), F32)], 0))
    bgl[0] = bs[0]
    bgl[1] = bs[1]
    for e in range(EXPERTS):
        c = 256 * e
        bs = split((gates[0][e] * back_mixed[0] + gates[1][e] * back_mixed[1]) * slopes[e])
        bpd[0, OUT * e : OUT * e + OUT, :] = bs[0]
        bpd[1, OUT * e : OUT * e + OUT, :] = bs[1]
        w = dn_b[c : c + 256, :]
        back = dot(w, jnp.concatenate([bs[0], bs[0]], 0), NN) + dot(w[:, 0:128], bs[1], NN)
        bs = split(back * dsu[c : c + 256, :])
        bpu[0, c : c + 256, :] = bs[0]
        bpu[1, c : c + 256, :] = bs[1]
    squares += sums

    class Piece:
        def __init__(self, c, base, size, expert):
            self.c, self.base, self.size, self.expert = c, base, size, expert
            one, two = ((bx, x_peer), (by, y_peer)) if c % 2 == 0 else ((by, y_peer), (bx, x_peer))
            self.b1, self.p1 = one
            self.b2, self.p2 = two
            self.o2 = base + self.b1 * (size // 2)
            self.o3 = self.o2 + self.b2 * (size // 4)
            self.part = size // 4 // nz
            self.o4 = self.o3 + mz * self.part

        def at(self, start, size):
            return pl.ds(pl.multiple_of(start, 8), size)

        def res(self, start, size):
            if self.expert:
                return gexp_ref.at[self.at(start, size)]
            return grep_ref.at[hid, self.at(start - rep_base, size)]

        def sems(self, k):
            return s_sem.at[6 * self.c + k], v_sem.at[6 * self.c + k]

        def core(self):
            rng = self.at(self.base, self.size)
            self.core_copy = remote(grads.at[1, rng], r_core.at[rng], *self.sems(0), core_peer)
            self.core_copy.start()

        def one(self):
            self.core_copy.wait()
            rng = self.at(self.base, self.size)
            grads[0, rng, :] += r_core[rng, :]
            half = self.size // 2
            src = self.at(self.base + (1 - self.b1) * half, half)
            self.copy = remote(grads.at[0, src], r_one.at[self.at(self.base // 2, half)], *self.sems(1), self.p1)
            self.copy.start()

        def two(self):
            self.copy.wait()
            half = self.size // 2
            grads[0, self.at(self.o2, half), :] += r_one[self.at(self.base // 2, half), :]
            quarter = self.size // 4
            src = self.at(self.o2 + (1 - self.b2) * quarter, quarter)
            self.copy = remote(grads.at[0, src], r_two.at[self.at(self.base // 4, quarter)], *self.sems(2), self.p2)
            self.copy.start()

        def z(self):
            self.copy.wait()
            quarter = self.size // 4
            grads[0, self.at(self.o3, quarter), :] += r_two[self.at(self.base // 4, quarter), :]
            self.z_copies = []
            q = self.c * (nz - 1)
            for k in range(1, nz):
                src = self.at(self.o3 + (mz + k) % nz * self.part, self.part)
                dst = r_z.at[nz - k - 1, self.at(self.base // (4 * nz), self.part)]
                sems = zs_sem.at[0, q + k - 1], zv_sem.at[0, q + nz - k - 1]
                self.z_copies.append(remote(grads.at[0, src], dst, *sems, z_peers[k - 1]))
            for copy in self.z_copies:
                copy.start()

        def zg(self):
            for copy in self.z_copies:
                copy.wait()
            total = grads[0, self.at(self.o4, self.part), :]
            for k in range(nz - 1):
                total = total + r_z[k, self.at(self.base // (4 * nz), self.part), :]
            out = self.res(self.o4, self.part)
            out[...] = total
            self.z_copies = []
            q = self.c * (nz - 1)
            for k in range(1, nz):
                sems = zs_sem.at[1, q + k - 1], zv_sem.at[1, q + nz - k - 1]
                self.z_copies.append(remote(out, out, *sems, z_peers[k - 1]))
            for copy in self.z_copies:
                copy.start()

        def twog(self):
            for copy in self.z_copies:
                copy.wait()
            out = self.res(self.o3, self.size // 4)
            self.copy = remote(out, out, *self.sems(3), self.p2)
            self.copy.start()

        def oneg(self):
            self.copy.wait()
            out = self.res(self.o2, self.size // 2)
            self.copy = remote(out, out, *self.sems(4), self.p1)
            self.copy.start()

        def coreg(self):
            self.copy.wait()
            if not self.expert:
                out = self.res(self.base, self.size)
                self.copy = remote(out, out, *self.sems(5), core_peer)
                self.copy.start()

        def end(self):
            if not self.expert:
                self.copy.wait()

    rep_base = chunks[EXPERTS][0][0]
    pieces = {}
    c = 0
    for k, (name, parts) in enumerate(zip(("e0", "e1", "e2", "e3", "i", "t"), chunks)):
        pieces[name] = []
        for base, size in parts:
            pieces[name].append(Piece(c, base, size, k < EXPERTS))
            c += 1

    def run(*steps):
        for step in steps:
            name, stage = step.split(".")
            for piece in pieces[name]:
                getattr(piece, stage)()

    def owner(k):
        return (k + hid) % 2

    e_base = [chunks[e][0][0] for e in range(EXPERTS)]
    e_size = chunks[1][0][0] - chunks[0][0][0]
    i_base, t_base = chunks[EXPERTS][0][0], chunks[EXPERTS + 1][0][0]
    t_size = grads.shape[1] - t_base
    misc = t_base + MISC_AT
    grads[:, misc : t_base + t_size, :] = jnp.zeros((2, t_size - MISC_AT, 128), F32)

    def expert_gradients(e):
        c, o, base = 256 * e, 128 * e, e_base[e]
        g = mm((x[0], x[1]), (bpu[0, c : c + 256, :], bpu[1, c : c + 256, :]), NT)
        grads[0, base : base + D, :] = g[0:D, 0:128]
        grads[1, base : base + D, :] = g[0:D, 128:256]
        upb = t_base + UPB_AT + e
        grads[0, upb : upb + 1, :] = g[D : D + 1, 0:128]
        grads[1, upb : upb + 1, :] = g[D : D + 1, 128:256]
        hi, lo = bpd[0, o : o + 128, :], bpd[1, o : o + 128, :]
        g = dot(h[0, c : c + 256, :], jnp.concatenate([hi, lo], 0), NT)
        g = (g[:, 0:128] + g[:, 128:256]) + dot(h[1, c : c + 256, :], hi, NT)
        grads[0, base + D : base + E_ROWS, :] = g[0:128]
        grads[1, base + D : base + E_ROWS, :] = g[128:256]
        if e_size > E_ROWS:
            grads[:, base + E_ROWS : base + e_size, :] = jnp.zeros((2, e_size - E_ROWS, 128), F32)
        run(f"e{e}.core")

    expert_gradients(0)
    expert_gradients(1)
    run("e0.one")
    expert_gradients(2)
    run("e1.one")
    expert_gradients(3)
    run("e2.one")

    def inputs_back(here):
        b = mm((up_b[0], up_b[1]), (bpu[0, :, here], bpu[1, :, here]))
        b = b + mm((gate_t[0, :, 0:16], gate_t[1, :, 0:16]), (bgl[0, :, here], bgl[1, :, here]))
        bs = split(b)
        bi[0, :, here] = bs[0]
        bi[1, :, here] = bs[1]
        ps = split(mm((w_in_b[0], w_in_b[1]), bs))
        bp[0, :, here] = ps[0]
        bp[1, :, here] = ps[1]

    inputs_back(slice(0, rows // 2))
    run("e3.one", "e0.two")
    inputs_back(slice(rows // 2, rows))
    run("e1.two")
    for k in range(2):
        g = mm((feat[0], feat[1]), (bi[0, 256 * k : 256 * k + 256, :], bi[1, 256 * k : 256 * k + 256, :]), NT)
        grads[owner(k), i_base : i_base + 432, :] = g[:, 0:128]
        grads[owner(k), i_base + 432 : i_base + I_ROWS, :] = g[:, 128:256]
    if t_base - i_base > I_ROWS:
        grads[:, i_base + I_ROWS : t_base, :] = jnp.zeros((2, t_base - i_base - I_ROWS, 128), F32)
    run("i.core", "e2.two", "e0.z")

    one16 = jnp.ones((16, rows), BF)
    g = mm((bgl[0], bgl[1]), (x[0], x[1]), NT)
    for k in range(4):
        at = t_base + GATE_AT + 8 * (k % 2)
        grads[owner(k // 2), at : at + 8, :] = g[0:8, 128 * k : 128 * k + 128]
    for t in range(TASKS):
        z = slice(TH * t, TH * t + TH)
        o = slice(OUT * t, OUT * t + OUT)
        g = mm((bpt[0, z, :], bpt[1, z, :]), (mixed[0, o, :], mixed[1, o, :]), NT)
        grads[owner(t), t_base + TOWER_AT : t_base + TOWER_AT + TH, :] = g
    lane = lax.broadcasted_iota(jnp.int32, (1, 128), 1)
    g = dot(one16, bpd[0], NT) + dot(one16, bpd[1], NT)
    m = owner(0)
    for e in range(EXPERTS):
        grads[m, misc + e : misc + e + 1, :] = g[0:1, 128 * e : 128 * e + 128]
    g = dot(one16, bpt[0], NT) + dot(one16, bpt[1], NT)
    grads[m, misc + 4 : misc + 5, :] = g[0:1]
    g = mm((thbl[0, 128:160, :], thbl[1, 128:160, :]), (thbl[0, 0:128, :], thbl[1, 0:128, :]), NT)
    grads[m, misc + 5 : misc + 6, :] = jnp.where(lane < TH, g[0:1], g[16:17])
    g = dot(one16, bgl[0], NT) + dot(one16, bgl[1], NT)
    grads[m, misc + 6 : misc + 7, 0:8] = g[0:1, 0:8]
    g = dot(one16, thbl[0, 128:160, :], NT) + dot(one16, thbl[1, 128:160, :], NT)
    grads[m, misc + 6 : misc + 7, 8:9] = g[0:1, 0:1]
    grads[m, misc + 6 : misc + 7, 9:10] = g[0:1, 16:17]
    total = jnp.zeros((1, 128), F32)
    for k in range(4):
        total = jnp.where(lane == k, squares[k], total)
    grads[m, misc + 7 : misc + 8, :] = total
    run("i.one", "e3.two", "e1.z")

    def table_fields(i, carry):
        for u in range(2):
            f = 2 * i + u
            at = pl.ds(pl.multiple_of(EMB * f, EMB), EMB)
            total = jnp.zeros((2 * EMB, VOCAB), F32)
            for j in range(rows // width):
                here = slice(width * j, width * (j + 1))
                back = jnp.concatenate([bp[0, at, here], bp[1, at, here]], 0)
                total = total + dot(back, bag_counts(part, f, here, width), NT)
            g = (total[0:EMB] + total[EMB : 2 * EMB]) * sixteen
            at = pl.ds(pl.multiple_of(t_base + EMB * f, EMB), EMB)
            grads[owner(0), at, :] = g[:, 0:128]
            grads[owner(1), at, :] = g[:, 128:256]
        return carry

    lax.fori_loop(0, 4, table_fields, 0)
    run("e2.z", "e0.zg")
    lax.fori_loop(4, 8, table_fields, 0)
    run("e3.z", "e1.zg", "i.two")
    lax.fori_loop(8, 13, table_fields, 0)
    run("t.core", "e0.twog", "e2.zg")
    run("t.one", "e1.twog", "e3.zg", "i.z", "e0.oneg", "e2.twog", "t.two", "e1.oneg", "e3.twog", "i.zg")
    run("t.z", "e2.oneg", "e3.oneg", "i.twog", "t.zg", "e0.coreg", "e1.coreg", "i.oneg", "t.twog", "e2.coreg")
    run("i.coreg", "t.oneg", "e3.coreg", "t.coreg", "i.end", "t.end")


def layout(n):
    unit = 8 * n
    chunks, base = [], 0
    for k, size in enumerate([E_ROWS] * EXPERTS + [I_ROWS, T_ROWS]):
        units = -(-size // unit)
        first = units if k < EXPERTS else (units + 1) // 2
        parts = [(base, first * unit)]
        if units > first:
            parts.append((base + first * unit, (units - first) * unit))
        chunks.append(parts)
        base += units * unit
    return chunks, base


def step(ids, lengths, dense, labels, tables, in_weight, up, down, up_bias, gate, tower, tower_out, biases, n, total_rows):
    rows = ids.shape[2] // 2
    chunks, size = layout(n)
    count = sum(len(parts) for parts in chunks)
    e_all = chunks[EXPERTS][0][0]
    nz = n // 4
    vm = pltpu.VMEM
    scratch = [
        vm((FIELDS, 4, rows), jnp.int32),
        vm((FIELDS, rows), jnp.int32),
        vm((13, rows), F32),
        vm((TASKS, rows), jnp.int32),
        vm((FIELDS, EMB, VOCAB), F32),
        vm((2, EXPERTS, D, 128), F32),
        vm((2, EXPERTS, 128, OUT), F32),
        vm((EXPERTS, 128), F32),
        vm((8, 1280), F32),
        vm((2, FIELDS, 4, rows), F32),
        vm((IN_ROWS, D), F32),
        vm((512, D), F32),
        vm((2, D, 512), BF),
        vm((2, POOLED, D), BF),
        vm((2, D, EXPERTS * HID), BF),
        vm((2, EXPERTS * HID + 16, D), BF),
        vm((EXPERTS * HID, 2 * OUT), BF),
        vm((2, EXPERTS, OUT, HID), BF),
        vm((TASKS * TH, 2 * OUT), BF),
        vm((2, D, 128), BF),
        vm((128, 128), F32),
        vm((128, 128), F32),
        vm((2, 432, rows), BF),
        vm((2, D + 16, rows), BF),
        vm((2, EXPERTS * HID, rows), BF),
        vm((2, EXPERTS * OUT, rows), BF),
        vm((2, EXPERTS * HID, rows), BF),
        vm((EXPERTS * HID, rows), F32),
        vm((2, TASKS * OUT, rows), BF),
        vm((2, TASKS * TH, rows), BF),
        vm((2, 16, rows), BF),
        vm((2, 160, rows), BF),
        vm((2, D, rows), BF),
        vm((2, POOLED, rows), BF),
        vm((2, size, 128), F32),
        vm((size, 128), F32),
        vm((size // 2, 128), F32),
        vm((size // 4, 128), F32),
        vm((nz - 1, size // n, 128), F32),
        pltpu.SemaphoreType.DMA((8,)),
        pltpu.SemaphoreType.DMA((3,)),
        pltpu.SemaphoreType.DMA((3,)),
        pltpu.SemaphoreType.DMA((6 * count,)),
        pltpu.SemaphoreType.DMA((6 * count,)),
        pltpu.SemaphoreType.DMA((2, count * (nz - 1))),
        pltpu.SemaphoreType.DMA((2, count * (nz - 1))),
    ]
    anywhere = pl.BlockSpec(memory_space=pl.ANY)
    local = pl.BlockSpec(memory_space=pltpu.VMEM)
    return pl.pallas_call(
        functools.partial(step_kernel, n, chunks, total_rows),
        out_shape=[
            jax.ShapeDtypeStruct((e_all, 128), F32),
            jax.ShapeDtypeStruct((2, size - e_all, 128), F32),
        ],
        in_specs=[anywhere] * 8 + [local] * 5,
        out_specs=[local] * 2,
        scratch_shapes=scratch,
        compiler_params=pltpu.CompilerParams(collective_id=0, has_side_effects=True, vmem_limit_bytes=62 << 20),
        name="step",
    )(ids, lengths, dense, labels, tables, in_weight, up, down, up_bias, gate, tower, tower_out, biases)


def update_kernel(e_size, i_size, counts, gexp_ref, grep_ref, *refs):
    *refs, row_ref = refs
    hid = lax.axis_index("hid")
    params = [refs[3 * k : 3 * k + 3] for k in range(9)]
    results = [refs[27 + 4 * k : 31 + 4 * k] for k in range(9)]
    rms_ref = refs[63]

    def update(k, at, g):
        w_ref, m_ref, a_ref = params[k]
        new_m = MOMENTUM_RATE * m_ref[at] + g
        new_w = w_ref[at] - LEARN_RATE * (g + MOMENTUM_RATE * new_m)
        ow, om, oa, orr = results[k]
        ow[at] = new_w
        om[at] = new_m
        oa[at] = AVERAGE_RATE * a_ref[at] + (1.0 - AVERAGE_RATE) * new_w
        orr[at] = new_w.astype(BF)

    t = i_size
    everything = slice(None)
    for f in range(FIELDS):
        for k in range(2):
            update(0, (f, everything, slice(128 * k, 128 * k + 128)), grep_ref[k, t + EMB * f : t + EMB * f + EMB, :])
    for k in range(4):
        at = 432 * (k % 2)
        update(1, (everything, slice(128 * k, 128 * k + 128)), grep_ref[k // 2, at : at + IN_ROWS, :])
    for e in range(EXPERTS):
        at = e_size * e
        update(2, (e,), gexp_ref[at : at + D, :])
        update(3, (e,), gexp_ref[at + D : at + E_ROWS, :])
    update(4, (everything,), grep_ref[hid, t + UPB_AT : t + UPB_AT + 4, :])
    for k in range(4):
        at = t + GATE_AT + 8 * (k % 2)
        for s in range(TASKS):
            g = grep_ref[k // 2, at + 4 * s : at + 4 * s + 4, :]
            update(5, (s, everything, slice(128 * k, 128 * k + 128)), g)
    for s in range(TASKS):
        update(6, (s,), grep_ref[s, t + TOWER_AT : t + TOWER_AT + TH, :])
    misc = t + MISC_AT
    tout = grep_ref[0, misc + 5 : misc + 6, :]
    for s in range(TASKS):
        update(7, (slice(s, s + 1), everything), tout[:, TH * s : TH * s + TH])
    for k in range(4):
        at = 432 * (k % 2) + IN_ROWS
        row_ref[0:1, 128 * k : 128 * k + 128] = grep_ref[k // 2, at : at + 1, :]
        row_ref[0:1, D + 128 * k : D + 128 * k + 128] = grep_ref[0, misc + k : misc + k + 1, :]
    row_ref[0:1, 1024:1032] = grep_ref[0, misc + 6 : misc + 7, 0:8]
    row_ref[0:1, 1032:1160] = grep_ref[0, misc + 4 : misc + 5, :]
    row_ref[0:1, 1160:1162] = grep_ref[0, misc + 6 : misc + 7, 8:10]
    update(8, (everything,), row_ref[0, 0:NB])
    squares = grep_ref[0, misc + 7 : misc + 8, :]
    lane = lax.broadcasted_iota(jnp.int32, (1, 128), 1)
    inverse = jnp.zeros((1, 128), F32)
    for k, count in enumerate(counts):
        inverse = jnp.where(lane == k, 1.0 / count, inverse)
    row_ref[1:2, 0:128] = jnp.sqrt(squares * inverse + 1e-06)
    rms_ref[...] = row_ref[1, 0:4]


def local(*args):
    n = lax.axis_size("dp")
    ids, lengths, dense, labels = args[:4]
    total_rows = ids.shape[0] * n
    params = [list(args[4 + 3 * k : 7 + 3 * k]) for k in range(9)]
    for k in (0, 5, 6):
        params[k] = [v.transpose(0, 2, 1) for v in params[k]]
    gexp, grep = step(
        ids.transpose(1, 2, 0),
        lengths.T,
        dense.T,
        labels.T,
        *[p[0] for p in params],
        n=n,
        total_rows=total_rows,
    )
    chunks, _ = layout(n)
    counts = [float(total_rows * c) for c in (D, EXPERTS * HID, EXPERTS * OUT, TASKS * TH)]
    shapes = []
    for p in params:
        shapes += [jax.ShapeDtypeStruct(p[0].shape, F32)] * 3 + [jax.ShapeDtypeStruct(p[0].shape, BF)]
    shapes.append(jax.ShapeDtypeStruct((4,), F32))
    flat = [v for p in params for v in p]
    vmem = pl.BlockSpec(memory_space=pltpu.VMEM)
    outs = pl.pallas_call(
        functools.partial(update_kernel, chunks[1][0][0], chunks[5][0][0] - chunks[4][0][0], counts),
        out_shape=shapes,
        in_specs=[vmem] * (2 + len(flat)),
        out_specs=[vmem] * len(shapes),
        scratch_shapes=[pltpu.VMEM((8, 1280), F32)],
        compiler_params=pltpu.CompilerParams(vmem_limit_bytes=62 << 20),
        name="update",
    )(gexp, grep, *flat)
    outs = list(outs)
    for k in (0, 5, 6):
        outs[4 * k : 4 * k + 4] = [v.transpose(0, 2, 1) for v in outs[4 * k : 4 * k + 4]]
    return tuple(outs)


def solution(mesh):
    up, down, bias = P(None, None, "hid"), P(None, "hid", None), P(None, "hid")
    rep = P()
    return jax.shard_map(
        local,
        mesh=mesh,
        in_specs=(P("dp", None, None), P("dp", None), P("dp", None), P("dp", None))
        + (rep,) * 6
        + (up,) * 3
        + (down,) * 3
        + (bias,) * 3
        + (rep,) * 12,
        out_specs=(rep,) * 8 + (up,) * 4 + (down,) * 4 + (bias,) * 4 + (rep,) * 17,
        check_vma=False,
    )
```

time: 154 us -> 93.1 us (0.60)
  Pallas kernels: 144 us -> 92 us
  other arithmetic: 5.22 us -> 0 us
  local copies, waits for them, and re-layouts: 3.88 us -> 0 us
    pallas_call x2, Pallas kernels: 144 us -> 92 us  [the longest x1 83.9 us: step(): pl.pallas_call(functools.partial(step_kernel, n, chunks, total_rows), out...]
    pallas_call x4 -> x0, other arithmetic: 5.22 us -> none  [local(): pl.pallas_call(functools.partial(update_kernel, padded(E_ROWS, n), padded...]
    reshape x3 -> x0, local copies, waits for them, and re-layouts: 3.88 us -> none  [local(): params[8] = [v.reshape(1, NB) for v in params[8]]]
where the time goes in v1:
time: 93.1 us; the launch traced here: 92.9 us
  Pallas kernels  92 us (99%)
    pallas_call x1, Pallas kernels, step(): pl.pallas_call(functools.partial(step_kernel, n, chunks, total_rows), out...  83.9 us
    pallas_call x1, Pallas kernels, local(): pl.pallas_call(functools.partial(update_kernel, chunks[1][0][0], chunks[5...  8.16 us

profile of v1, /device:TPU:0, one launch (start us, length us, event | category | flops | bytes accessed | tf_op | source)
XLA Modules:
  0.0 92.9 jit_solution(16980929790289052090)
XLA Ops:
  0.7 83.9 %step.1 = (f32[2560,128]{1,0:T(8,128)}, f32[2,1408,128]{2,1,0:T(8,128)}) custom-call(s32[26,4,2048]{2,1,0:T(4,128)} %bitcast.27, s32[26,2048]{1,0:T(8,128)} %bitcast.32, f32[13,2048]{1,0:T(8,128)} %bitcast.33, s32[2,2048]{1,0:T(2,128)} %bitcast.38, f32[26,16,256]{2,1,0:T(8,128)} %bitcast.25, f32[429,512]{1,0:T(8,128)} %refs_3_.1, f32[4,512,128]{2,1,0:T(8,128)} %refs_6_.1, ...), custom_call_target="tpu_custom_call" | custom-call | tf_op jit(solution)/shard_map/step/pallas_call | solution.py:666
  84.6 8.2 %update.1 = (f32[26,16,256]{2,1,0:T(8,128)}, f32[26,16,256]{2,1,0:T(8,128)}, f32[26,16,256]{2,1,0:T(8,128)}, bf16[26,16,256]{2,1,0:T(8,128)(2,1)}, f32[429,512]{...) custom-call(f32[2560,128]{1,0:T(8,128)} %get-tuple-element.76.gexp_r, ...), custom_call_target="tpu_custom_call" | custom-call | tf_op jit(solution)/shard_map/update/pallas_call | solution.py:762

commit v2 on v1

v2 whole, which is shorter than its diff:
```python
import functools

import jax
import jax.numpy as jnp
from jax import lax
from jax.experimental import pallas as pl
from jax.experimental.pallas import tpu as pltpu
from jax.sharding import PartitionSpec as P

D = 512
HID = 256
OUT = 128
TH = 64
TASKS = 2
EXPERTS = 4
FIELDS = 26
VOCAB = 256
EMB = 16
POOLED = 416
IN_ROWS = 429
NB = 1162

MOMENTUM_RATE = 0.9
LEARN_RATE = 0.3
AVERAGE_RATE = 0.9

BF = jnp.bfloat16
F32 = jnp.float32
NN = (((1,), (0,)), ((), ()))
NT = (((1,), (1,)), ((), ()))
MESH = pl.DeviceIdType.MESH

E_ROWS = 640
I_BASE = EXPERTS * E_ROWS
I_ROWS = 864
GATE_AT = 416
TOWER_AT = 432
MISC_AT = 496
UPB_AT = 504
T_ROWS = 512


PARTS = (
    ((640, "xyz"),),
    ((640, "yxz"),),
    ((640, "pz"),),
    ((640, "pz"),),
    ((512, "pz"), (384, "zxy"),),
    ((512, "pz"),),
)
SCHEDULE = (
    "!b2",
    "!b3",
    "!G2",
    "!D2",
    "e2a",
    "!G3",
    "e2a",
    "!D3",
    "e3a",
    "!b0",
    "!b1",
    "!G0",
    "e3a",
    "!D0",
    "e0a",
    "!G1",
    "e0a",
    "!D1",
    "e1a",
    "!s0",
    "e2a e1a",
    "!h0",
    "e3a",
    "!i0",
    "e2a",
    "!i1",
    "ib e1a ia e0a",
    "!h1",
    "ia ib",
    "!j0-7",
    "e1a e0a e2a",
    "!j7-13",
    "e3a ia ta ib",
    "ta e1a e2a u2",
    "ib e0a e3a ib",
    "ia ta e1a e0a",
    "ib ia e3a u3",
    "ta e1a e0a ib",
    "ia ta ia e1a",
    "e0a u1 u0 ib",
    "ib ui ta ta",
    "ur",
)


def split(v):
    hi = v.astype(BF)
    return hi, (v - hi.astype(F32)).astype(BF)


def dot(a, b, dims):
    return lax.dot_general(a, b, dims, preferred_element_type=F32)


def mm(a, b, dims=NN):
    return dot(a[0], b[0], dims) + (dot(a[1], b[0], dims) + dot(a[0], b[1], dims))


def bag_counts(part_ref, f, here, width):
    row = lax.broadcasted_iota(jnp.int32, (16, width), 0).astype(F32).astype(BF)
    zero = jnp.zeros((16, width), BF)
    weights = [jnp.broadcast_to(part_ref[0, f, s : s + 1, here], (16, width)).astype(BF) for s in range(4)]
    offsets = [jnp.broadcast_to(part_ref[1, f, s : s + 1, here], (16, width)).astype(BF) - row for s in range(4)]
    low, high = [], []
    for t in range(8):
        start = jnp.full((16, width), 16 * t, BF)
        hit = [jnp.where(offsets[s] == start, weights[s], zero) for s in range(4)]
        both = (hit[0] + hit[1]) + (hit[2] + hit[3])
        whole = (both + 128.0) - 128.0
        low.append(both - whole)
        high.append(whole)
    return jnp.concatenate(low + high, 0)


def step_kernel(n, chunks, total_rows, counts, *refs):
    hbm, refs = refs[:31], refs[31:]
    outs, refs = refs[:37], refs[37:]
    ids_hbm, len_hbm, dense_hbm, lab_hbm = hbm[:4]
    up_hbm, dn_hbm, upb_hbm = hbm[10], hbm[13], hbm[16]
    params = [outs[4 * k : 4 * k + 4] for k in range(9)]
    rms_ref = outs[36]
    tab_ref, w_raw, upo_ref, dno_ref, upbo_ref, gate_ref, tw_ref, tout_ref, bias_ref = [p[0] for p in params]
    (
        ids_ref,
        len_ref,
        dense_ref,
        lab_ref,
        upx_ref,
        dnx_ref,
        upbx_ref,
        brow,
        part,
        w_in,
        w_in_t,
        w_in_b,
        up_b,
        up_t,
        dn_b,
        dn_t,
        tw_b,
        gate_t,
        cols,
        bcol,
        feat,
        x,
        h,
        bpd,
        bpu,
        dsu,
        mixed,
        bpt,
        bgl,
        row_sums,
        bi,
        bp,
        grads,
        total_e,
        total_r,
        r_core,
        r_sum,
        in_sem,
        w_send,
        w_recv,
        s_sem,
        v_sem,
    ) = refs
    dp = lax.axis_index("dp")
    hid = lax.axis_index("hid")
    core_peer = (dp, 1 - hid)

    def group(stride, size):
        me = dp // stride % size
        others = [(me + k) % size for k in range(1, size)]
        return me, [(q, (dp + (q - me) * stride, hid)) for q in others]

    groups = {"x": group(1, 2), "y": group(2, 2), "z": group(4, n // 4), "p": group(1, 4), "a": group(1, n)}

    barrier = pltpu.get_barrier_semaphore()
    everyone = [core_peer] + [peer for _, peer in groups["a"][1]]
    for peer in everyone:
        pl.semaphore_signal(barrier, inc=1, device_id=peer, device_id_type=MESH)

    rows = ids_ref.shape[2]
    lanes = pl.ds(pl.multiple_of(hid * rows, rows), rows)
    order = (0, 1, 2, 3, 4, 5, 6, 7, 8)
    pairs = [(ids_hbm.at[:, :, lanes], ids_ref), (len_hbm.at[:, lanes], len_ref)]
    pairs += [(hbm[4 + 3 * k], params[k][0]) for k in order]
    pairs += [(dense_hbm.at[:, lanes], dense_ref), (lab_hbm.at[:, lanes], lab_ref)]
    for j in (1, 2):
        pairs += [(hbm[4 + 3 * k + j], params[k][j]) for k in order]
    loads = [pltpu.make_async_copy(src, dst, in_sem.at[k]) for k, (src, dst) in enumerate(pairs)]
    for load in loads[:13]:
        load.start()

    def remote(src, dst, send, recv, peer):
        return pltpu.make_async_remote_copy(
            src_ref=src, dst_ref=dst, send_sem=send, recv_sem=recv, device_id=peer, device_id_type=MESH
        )

    pl.semaphore_wait(barrier, len(everyone))
    weights = [
        remote(src, dst, w_send.at[k], w_recv.at[k], core_peer)
        for k, (src, dst) in enumerate(((up_hbm, upx_ref), (dn_hbm, dnx_ref), (upb_hbm, upbx_ref)))
    ]
    for copy in weights:
        copy.start()

    loads[0].wait()
    loads[1].wait()
    slot = lax.broadcasted_iota(jnp.int32, (4, rows), 0)
    for f in range(FIELDS):
        used = jnp.broadcast_to(len_ref[f : f + 1, :], (4, rows)) > slot
        ident = ids_ref[f]
        part[0, f] = jnp.where(used, jnp.where(ident < 128, 0.0625, 1.0), 0.0)
        part[1, f] = jnp.bitwise_and(ident, 127).astype(F32)
    for load in loads[2:13]:
        load.wait()

    sixteen = jnp.where(lax.broadcasted_iota(jnp.int32, (EMB, VOCAB), 1) < 128, 16.0, 1.0)
    width = 256

    def pool_fields(i, carry):
        for u in range(2):
            f = 2 * i + u
            table = jnp.concatenate(split(tab_ref[f] * sixteen), 0)
            at = pl.ds(pl.multiple_of(EMB * f, EMB), EMB)
            for j in range(rows // width):
                here = slice(width * j, width * (j + 1))
                both = dot(table, bag_counts(part, f, here, width), NN)
                hi, lo = split(both[0:EMB] + both[EMB : 2 * EMB])
                feat[0, at, here] = hi
                feat[1, at, here] = lo
        return carry

    lax.fori_loop(0, FIELDS // 2, pool_fields, 0)
    for load in loads[13:]:
        load.start()

    brow[0:1, 0:1024] = bias_ref[0:1024].reshape(1, 1024)
    brow[0:1, 1024:NB] = bias_ref[1024:NB].reshape(1, NB - 1024)
    biases = brow[0:1, 0:NB]
    row = lax.broadcasted_iota(jnp.int32, (8, D), 0)
    in_bias = jnp.broadcast_to(biases[:, 0:D], (8, D))
    w_in[0:IN_ROWS, :] = w_raw[...]
    w_in[424:432, :] = jnp.where(row == 5, in_bias, jnp.where(row < 5, w_in[424:432, :], 0.0))
    w_in[432:512, :] = jnp.zeros((80, D), F32)
    for i in range(4):
        hi, lo = split(w_in[128 * i : 128 * (i + 1), :].T)
        w_in_t[0, :, 128 * i : 128 * (i + 1)] = hi
        w_in_t[1, :, 128 * i : 128 * (i + 1)] = lo
    hi, lo = split(w_in[0:POOLED, :])
    w_in_b[0] = hi
    w_in_b[1] = lo

    def expert_weights(k, up_ref, dn_ref):
        for e in range(EXPERTS):
            c = 256 * e + 128 * k
            up, down = up_ref[e], dn_ref[e]
            hi, lo = split(up)
            up_b[0, :, c : c + 128] = hi
            up_b[1, :, c : c + 128] = lo
            hi, lo = split(up.T)
            up_t[0, c : c + 128, :] = hi
            up_t[1, c : c + 128, :] = lo
            hi, lo = split(down)
            dn_b[c : c + 128, 0:128] = hi
            dn_b[c : c + 128, 128:256] = lo
            hi, lo = split(down.T)
            dn_t[0, e, :, 128 * k : 128 * k + 128] = hi
            dn_t[1, e, :, 128 * k : 128 * k + 128] = lo

    expert_weights(0, upo_ref, dno_ref)
    gate8 = jnp.concatenate([gate_ref[0], gate_ref[1]], 0)
    hi, lo = split(jnp.concatenate([gate8, jnp.zeros((8, D), F32)], 0))
    up_t[0, 1024:1040, :] = hi
    up_t[1, 1024:1040, :] = lo
    for i in range(4):
        tile = jnp.concatenate([gate8[:, 128 * i : 128 * (i + 1)], jnp.zeros((120, 128), F32)], 0).T
        hi, lo = split(tile)
        at = slice(128 * i, 128 * (i + 1))
        gate_t[at, 0:16] = hi[:, 0:16]
        gate_t[at, 16:32] = hi[:, 0:16]
        gate_t[at, 32:48] = lo[:, 0:16]
    for t in range(TASKS):
        hi, lo = split(tw_ref[t])
        tw_b[TH * t : TH * t + TH, 0:128] = hi
        tw_b[TH * t : TH * t + TH, 128:256] = lo
    tw_t = split(jnp.concatenate([tw_ref[0], tw_ref[1]], 0).T)
    x[0, D : D + 16, :] = jnp.ones((16, rows), BF)
    x[1, D : D + 16, :] = jnp.zeros((16, rows), BF)
    hi, lo = split(jnp.concatenate([dense_ref[...], jnp.ones((1, rows), F32), jnp.zeros((2, rows), F32)], 0))
    feat[0, POOLED:432, :] = hi
    feat[1, POOLED:432, :] = lo

    for copy in weights:
        copy.wait_recv()
    expert_weights(1, upx_ref, dnx_ref)
    bcol[...] = jnp.zeros((128, 128), F32)
    bcol[0:4, :] = upbo_ref[...]
    bcol[4:8, :] = upbx_ref[...]
    for e in range(EXPERTS):
        bcol[8 + e : 9 + e, :] = biases[:, 512 + 128 * e : 640 + 128 * e]
    bcol[12:13, :] = biases[:, 1032:1160]
    bcol[13:14, 0:64] = tout_ref[0:1, :]
    bcol[13:14, 64:128] = tout_ref[1:2, :]
    bcol[14:15, 0:8] = biases[:, 1024:1032]
    cols[...] = bcol[...].T
    row_sums[...] = jnp.zeros((128, 128), F32)

    scale = float(total_rows) ** -0.5
    fs = (feat[0], feat[1])
    xv = mm((w_in_t[0, :, 0:432], w_in_t[1, :, 0:432]), fs)
    squares = [jnp.sum(xv * xv, keepdims=True)]
    xs = split(xv)
    x[0, 0:D, :] = xs[0]
    x[1, 0:D, :] = xs[1]
    eouts, slopes = [], []
    sums = [0.0, 0.0, 0.0]
    for e in range(EXPERTS):
        c = 256 * e
        end = c + 256 if e < EXPERTS - 1 else c + 272
        pre = mm((up_t[0, c:end, :], up_t[1, c:end, :]), xs)
        gate_logits = pre[256:264] + cols[0:8, 14:15] if e == EXPERTS - 1 else None
        pre = pre[0:256] + jnp.concatenate([cols[:, e : e + 1], cols[:, 4 + e : 5 + e]], 0)
        s = jax.nn.sigmoid(pre)
        hv = pre * s
        dsu[c : c + 256, :] = s + hv * (1.0 - s)
        sums[0] = sums[0] + jnp.sum(hv * hv, keepdims=True)
        hs = split(hv)
        h[0, c : c + 256, :] = hs[0]
        h[1, c : c + 256, :] = hs[1]
        pre = mm((dn_t[0, e], dn_t[1, e]), hs) + cols[:, 8 + e : 9 + e]
        s = jax.nn.sigmoid(pre)
        out = pre * s
        sums[1] = sums[1] + jnp.sum(out * out, keepdims=True)
        eouts.append(out)
        slopes.append(s + out * (1.0 - s))
    gates = []
    for t in range(TASKS):
        r = [gate_logits[4 * t + e : 4 * t + e + 1] for e in range(EXPERTS)]
        top = jnp.maximum(jnp.maximum(r[0], r[1]), jnp.maximum(r[2], r[3]))
        ex = [jnp.exp(v - top) for v in r]
        inv = 1.0 / ((ex[0] + ex[1]) + (ex[2] + ex[3]))
        gates.append([v * inv for v in ex])
    back_mixed, back_logit = [], []
    for t in range(TASKS):
        z = slice(TH * t, TH * t + TH)
        o = slice(OUT * t, OUT * t + OUT)
        g = gates[t]
        ms = split(g[0] * eouts[0] + g[1] * eouts[1] + g[2] * eouts[2] + g[3] * eouts[3])
        mixed[t, 0:OUT, :] = ms[0]
        mixed[t, OUT : 2 * OUT, :] = ms[1]
        w = tw_b[z, :]
        pre = dot(w, jnp.concatenate([ms[0], ms[0]], 0), NN) + dot(w[:, 0:128], ms[1], NN) + cols[z, 12:13]
        s = jax.nn.sigmoid(pre)
        th = pre * s
        sums[2] = sums[2] + jnp.sum(th * th, keepdims=True)
        wo = cols[z, 13:14]
        logit = jnp.sum(th * wo, axis=0, keepdims=True) + biases[:, 1160 + t : 1161 + t]
        back = (jax.nn.sigmoid(logit) - lab_ref[t : t + 1, :].astype(F32)) * scale
        row_sums[z, 5:6] = jnp.sum(back * th, axis=1, keepdims=True)
        row_sums[8 + t : 9 + t, 6:7] = jnp.sum(back, axis=1, keepdims=True)
        back = back * wo * (s + th * (1.0 - s))
        row_sums[z, 4:5] = jnp.sum(back, axis=1, keepdims=True)
        bs = split(back)
        bpt[t, 0:TH, :] = bs[0]
        bpt[t, TH : 2 * TH, :] = bs[1]
        w = [v[:, z] for v in tw_t]
        bm = dot(jnp.concatenate([w[0], w[1], w[0]], 1), jnp.concatenate([bs[0], bs[0], bs[1]], 0), NN)
        back_mixed.append(bm)
        bg = [jnp.sum(bm * eouts[e], axis=0, keepdims=True) for e in range(EXPERTS)]
        mean = g[0] * bg[0] + g[1] * bg[1] + g[2] * bg[2] + g[3] * bg[3]
        back_logit += [g[e] * (bg[e] - mean) for e in range(EXPERTS)]
    back_logit = jnp.concatenate(back_logit, 0)
    row_sums[0:8, 6:7] = jnp.sum(back_logit, axis=1, keepdims=True)
    bs = split(jnp.concatenate([back_logit, jnp.zeros((8, rows), F32)], 0))
    bgl[0:16] = bs[0]
    bgl[16:32] = bs[1]
    bgl[32:48] = bs[0]
    squares += sums

    def expert_back(e):
        c = 256 * e
        back = (gates[0][e] * back_mixed[0] + gates[1][e] * back_mixed[1]) * slopes[e]
        row_sums[:, e : e + 1] = jnp.sum(back, axis=1, keepdims=True)
        bs = split(back)
        bpd[0, OUT * e : OUT * e + OUT, :] = bs[0]
        bpd[1, OUT * e : OUT * e + OUT, :] = bs[1]
        w = dn_b[c : c + 256, :]
        back = dot(w, jnp.concatenate([bs[0], bs[0]], 0), NN) + dot(w[:, 0:128], bs[1], NN)
        bs = split(back * dsu[c : c + 256, :])
        bpu[0, c : c + 256, :] = bs[0]
        bpu[1, c : c + 256, :] = bs[1]

    rep_base = chunks[EXPERTS][0][0]
    sent = []
    used = {"sem": 0, "row": 0}

    def sems(count):
        first = used["sem"]
        used["sem"] += count
        return first

    class Piece:
        def __init__(self, base, size, steps, expert):
            self.base, self.size, self.expert = base, size, expert
            self.steps = [groups[k] for k in steps]
            self.plan = self.stages()

        def at(self, start, size):
            return pl.ds(pl.multiple_of(start, 8), size)

        def total(self, start, size):
            if self.expert:
                return total_e.at[self.at(start, size)]
            return total_r.at[hid, self.at(start - rep_base, size)]

        def start(self, copies):
            for copy in copies:
                copy.start()
            sent.extend(copies)
            return copies

        def stages(self):
            rng = self.at(self.base, self.size)
            k = sems(1)
            yield self.start([remote(grads.at[1, rng], r_core.at[rng], s_sem.at[k], v_sem.at[k], core_peer)])
            grads[0, rng, :] += r_core[rng, :]
            start, size, held = self.base, self.size, []
            for me, others in self.steps:
                m = len(others) + 1
                held.append((start, size))
                size //= m
                k, row = sems(m - 1), used["row"]
                used["row"] += (m - 1) * size
                copies = []
                for j, (q, peer) in enumerate(others):
                    slot = m - 2 - j
                    src, dst = self.at(start + q * size, size), self.at(row + slot * size, size)
                    copies.append(remote(grads.at[0, src], r_sum.at[dst], s_sem.at[k + j], v_sem.at[k + slot], peer))
                yield self.start(copies)
                start = start + me * size
                mine = self.at(start, size)
                total = grads[0, mine, :]
                for slot in range(m - 1):
                    total = total + r_sum[row + slot * size : row + slot * size + size, :]
                if len(held) < len(self.steps):
                    grads[0, mine, :] = total
                else:
                    self.total(start, size)[...] = total
            for me, others in reversed(self.steps):
                m = len(others) + 1
                out = self.total(start, size)
                k = sems(m - 1)
                yield self.start(
                    [remote(out, out, s_sem.at[k + j], v_sem.at[k + m - 2 - j], peer) for j, (_, peer) in enumerate(others)]
                )
                start, size = held.pop()
            if not self.expert:
                out = self.total(self.base, self.size)
                k = sems(1)
                yield self.start([remote(out, out, s_sem.at[k], v_sem.at[k], core_peer)])

        def advance(self):
            for copy in getattr(self, "copies", []):
                copy.wait_recv()
            self.copies = next(self.plan, [])

    names = ("e0", "e1", "e2", "e3", "i", "t")
    pieces = {}
    for k, (name, parts) in enumerate(zip(names, chunks)):
        for j, (base, size, steps) in enumerate(parts):
            pieces[name + "abcd"[j]] = Piece(base, size, steps, k < EXPERTS)

    def owner(k):
        return (k + hid) % 2

    e_base = [chunks[e][0][0] for e in range(EXPERTS)]
    e_size = chunks[1][0][0] - chunks[0][0][0]
    i_base, t_base = chunks[EXPERTS][0][0], chunks[EXPERTS + 1][0][0]
    t_size = grads.shape[1] - t_base
    misc = t_base + MISC_AT
    grads[:, misc : t_base + t_size, :] = jnp.zeros((2, t_size - MISC_AT, 128), F32)

    def update(k, at, g):
        w_ref, m_ref, a_ref, r_ref = params[k]
        new_m = MOMENTUM_RATE * m_ref[at] + g
        new_w = w_ref[at] - LEARN_RATE * (g + MOMENTUM_RATE * new_m)
        w_ref[at] = new_w
        m_ref[at] = new_m
        a_ref[at] = AVERAGE_RATE * a_ref[at] + (1.0 - AVERAGE_RATE) * new_w
        r_ref[at] = new_w.astype(BF)

    everything = slice(None)
    to = t_base - rep_base

    def update_expert(e):
        update(2, (e,), total_e[e_base[e] : e_base[e] + D, :])
        update(3, (e,), total_e[e_base[e] + D : e_base[e] + E_ROWS, :])

    def update_inputs():
        for k in range(4):
            at = 432 * (k % 2)
            update(1, (everything, slice(128 * k, 128 * k + 128)), total_r[k // 2, at : at + IN_ROWS, :])

    def update_tables(first, last):
        for f in range(first, last):
            for k in range(2):
                g = total_r[k, to + EMB * f : to + EMB * f + EMB, :]
                update(0, (f, everything, slice(128 * k, 128 * k + 128)), g)

    def update_rest():
        update(4, (everything,), total_r[hid, to + UPB_AT : to + UPB_AT + 4, :])
        for k in range(4):
            at = to + GATE_AT + 8 * (k % 2)
            for s in range(TASKS):
                g = total_r[k // 2, at + 4 * s : at + 4 * s + 4, :]
                update(5, (s, everything, slice(128 * k, 128 * k + 128)), g)
        for s in range(TASKS):
            update(6, (s,), total_r[s, to + TOWER_AT : to + TOWER_AT + TH, :])
        at = to + MISC_AT
        g = total_r[0, at + 5 : at + 6, :]
        for s in range(TASKS):
            update(7, (slice(s, s + 1), everything), g[:, TH * s : TH * s + TH])
        for k in range(4):
            r = 432 * (k % 2) + IN_ROWS
            brow[0:1, 128 * k : 128 * k + 128] = total_r[k // 2, r : r + 1, :]
            brow[0:1, D + 128 * k : D + 128 * k + 128] = total_r[0, at + k : at + k + 1, :]
        brow[0:1, 1024:1032] = total_r[0, at + 6 : at + 7, 0:8]
        brow[0:1, 1032:1160] = total_r[0, at + 4 : at + 5, :]
        brow[0:1, 1160:1162] = total_r[0, at + 6 : at + 7, 8:10]
        update(8, (everything,), brow[0, 0:NB])
        lane = lax.broadcasted_iota(jnp.int32, (1, 128), 1)
        inverse = jnp.zeros((1, 128), F32)
        for k, count in enumerate(counts):
            inverse = jnp.where(lane == k, 1.0 / count, inverse)
        brow[1:2, 0:128] = jnp.sqrt(total_r[0, at + 7 : at + 8, :] * inverse + 1e-06)
        rms_ref[...] = brow[1, 0:4]

    updates = {f"u{e}": functools.partial(update_expert, e) for e in range(EXPERTS)}
    table_split = FIELDS if len(chunks[5]) == 1 else min(FIELDS, sum(part[1] for part in chunks[5][:-1]) // EMB)
    updates["ui"] = update_inputs
    updates["ut"] = functools.partial(update_tables, 0, table_split)
    updates["ur"] = lambda: (update_tables(table_split, FIELDS), update_rest())

    done = set()

    def run(*steps):
        for name in steps:
            if name in updates:
                if not done:
                    for load in loads[13:]:
                        load.wait()
                done.add(name)
                updates[name]()
            elif name in pieces:
                pieces[name].advance()

    def first_gradients(e):
        c, base = 256 * e, e_base[e]
        g = mm((x[0], x[1]), (bpu[0, c : c + 256, :], bpu[1, c : c + 256, :]), NT)
        grads[0, base : base + D, :] = g[0:D, 0:128]
        grads[1, base : base + D, :] = g[0:D, 128:256]
        upb = t_base + UPB_AT + e
        grads[0, upb : upb + 1, :] = g[D : D + 1, 0:128]
        grads[1, upb : upb + 1, :] = g[D : D + 1, 128:256]

    def second_gradients(e):
        c, o, base = 256 * e, 128 * e, e_base[e]
        hi, lo = bpd[0, o : o + 128, :], bpd[1, o : o + 128, :]
        g = dot(h[0, c : c + 256, :], jnp.concatenate([hi, lo], 0), NT)
        g = (g[:, 0:128] + g[:, 128:256]) + dot(h[1, c : c + 256, :], hi, NT)
        grads[0, base + D : base + E_ROWS, :] = g[0:128]
        grads[1, base + D : base + E_ROWS, :] = g[128:256]
        if e_size > E_ROWS:
            grads[:, base + E_ROWS : base + e_size, :] = jnp.zeros((2, e_size - E_ROWS, 128), F32)

    def inputs_back(k):
        if k == 0:
            b = mm((up_b[0], up_b[1]), (bpu[0], bpu[1])) + dot(gate_t[...], bgl[...], NN)
            bs = split(b)
            bi[0] = bs[0]
            bi[1] = bs[1]
        else:
            ps = split(mm((w_in_b[0], w_in_b[1]), (bi[0], bi[1])))
            bp[0] = ps[0]
            bp[1] = ps[1]

    def input_gradients(k):
        g = mm((feat[0], feat[1]), (bi[0, 256 * k : 256 * k + 256, :], bi[1, 256 * k : 256 * k + 256, :]), NT)
        grads[owner(k), i_base : i_base + 432, :] = g[:, 0:128]
        grads[owner(k), i_base + 432 : i_base + I_ROWS, :] = g[:, 128:256]
        if t_base - i_base > I_ROWS:
            grads[:, i_base + I_ROWS : t_base, :] = jnp.zeros((2, t_base - i_base - I_ROWS, 128), F32)

    def small_gradients():
        g = dot(x[0], bgl[0:32], NT)
        g = g[0:D, 0:8] + g[0:D, 16:24] + dot(x[1], bgl[0:16], NT)[0:D, 0:8]
        for k in range(4):
            tile = jnp.concatenate([g[128 * k : 128 * k + 128], jnp.zeros((128, 120), F32)], 1).T
            at = t_base + GATE_AT + 8 * (k % 2)
            grads[owner(k // 2), at : at + 8, :] = tile[0:8]
        for t in range(TASKS):
            g = dot(bpt[t], mixed[t], NT)
            g = (g[0:TH, 0:OUT] + g[0:TH, OUT : 2 * OUT]) + g[TH : 2 * TH, 0:OUT]
            grads[owner(t), t_base + TOWER_AT : t_base + TOWER_AT + TH, :] = g
        lane = lax.broadcasted_iota(jnp.int32, (1, 128), 1)
        m = owner(0)
        grads[m, misc : misc + 8, :] = row_sums[...].T[0:8]
        total = jnp.zeros((1, 128), F32)
        for k in range(4):
            total = jnp.where(lane == k, squares[k], total)
        grads[m, misc + 7 : misc + 8, :] = total

    def table_fields(i, carry):
        for u in range(2):
            f = 2 * i + u
            at = pl.ds(pl.multiple_of(EMB * f, EMB), EMB)
            total = jnp.zeros((2 * EMB, VOCAB), F32)
            for j in range(rows // width):
                here = slice(width * j, width * (j + 1))
                back = jnp.concatenate([bp[0, at, here], bp[1, at, here]], 0)
                total = total + dot(back, bag_counts(part, f, here, width), NT)
            g = (total[0:EMB] + total[EMB : 2 * EMB]) * sixteen
            at = pl.ds(pl.multiple_of(t_base + EMB * f, EMB), EMB)
            grads[owner(0), at, :] = g[:, 0:128]
            grads[owner(1), at, :] = g[:, 128:256]
        return carry

    def tables(first, last):
        lax.fori_loop(first, last, table_fields, 0)

    work = {
        "b": expert_back,
        "G": first_gradients,
        "D": second_gradients,
        "h": inputs_back,
        "i": input_gradients,
        "s": lambda k: small_gradients(),
    }
    for item in SCHEDULE:
        if item[0:2] == "!j":
            tables(*[int(v) for v in item[2:].split("-")])
        elif item[0] == "!":
            work[item[1]](int(item[2]))
        else:
            run(*item.split())
    while any(piece.copies for piece in pieces.values()):
        run(*[name for name in pieces if pieces[name].copies])
    run(*[name for name in updates if name not in done])
    for copy in sent + weights:
        copy.wait_send()


def layout(n):
    unit = 8 * n
    chunks, base = [], 0
    for size, parts in zip([E_ROWS] * EXPERTS + [I_ROWS, T_ROWS], PARTS):
        left = -(-size // unit) * unit
        pieces = []
        for j, (rows, steps) in enumerate(parts):
            take = left if j == len(parts) - 1 else min(left, -(-rows // unit) * unit)
            if take:
                pieces.append((base, take, steps))
            base += take
            left -= take
        chunks.append(pieces)
    return chunks, base


def step(args, shapes, n, total_rows):
    rows = args[0].shape[2] // 2
    chunks, size = layout(n)
    e_all = chunks[EXPERTS][0][0]
    count = 0
    for parts in chunks:
        for _, _, steps in parts:
            count += 2 + 2 * sum({"x": 1, "y": 1, "p": 3, "z": n // 4 - 1, "a": n - 1}[k] for k in steps)
    vm = pltpu.VMEM
    scratch = [
        vm((FIELDS, 4, rows), jnp.int32),
        vm((FIELDS, rows), jnp.int32),
        vm((13, rows), F32),
        vm((TASKS, rows), jnp.int32),
        vm((EXPERTS, D, 128), F32),
        vm((EXPERTS, 128, OUT), F32),
        vm((EXPERTS, 128), F32),
        vm((8, 1280), F32),
        vm((2, FIELDS, 4, rows), F32),
        vm((512, D), F32),
        vm((2, D, 512), BF),
        vm((2, POOLED, D), BF),
        vm((2, D, EXPERTS * HID), BF),
        vm((2, EXPERTS * HID + 16, D), BF),
        vm((EXPERTS * HID, 2 * OUT), BF),
        vm((2, EXPERTS, OUT, HID), BF),
        vm((TASKS * TH, 2 * OUT), BF),
        vm((D, 48), BF),
        vm((128, 128), F32),
        vm((128, 128), F32),
        vm((2, 432, rows), BF),
        vm((2, D + 16, rows), BF),
        vm((2, EXPERTS * HID, rows), BF),
        vm((2, EXPERTS * OUT, rows), BF),
        vm((2, EXPERTS * HID, rows), BF),
        vm((EXPERTS * HID, rows), F32),
        vm((TASKS, 2 * OUT, rows), BF),
        vm((TASKS, 2 * TH, rows), BF),
        vm((48, rows), BF),
        vm((128, 128), F32),
        vm((2, D, rows), BF),
        vm((2, POOLED, rows), BF),
        vm((2, size, 128), F32),
        vm((e_all, 128), F32),
        vm((2, size - e_all, 128), F32),
        vm((size, 128), F32),
        vm((size, 128), F32),
        pltpu.SemaphoreType.DMA((31,)),
        pltpu.SemaphoreType.DMA((3,)),
        pltpu.SemaphoreType.DMA((3,)),
        pltpu.SemaphoreType.DMA((count,)),
        pltpu.SemaphoreType.DMA((count,)),
    ]
    counts = [float(total_rows * c) for c in (D, EXPERTS * HID, EXPERTS * OUT, TASKS * TH)]
    return pl.pallas_call(
        functools.partial(step_kernel, n, chunks, total_rows, counts),
        out_shape=[pltpu.VMEM(shape, dtype) for shape, dtype in shapes],
        in_specs=[pl.BlockSpec(memory_space=pl.ANY)] * len(args),
        out_specs=[pl.BlockSpec(memory_space=pltpu.VMEM)] * len(shapes),
        scratch_shapes=scratch,
        compiler_params=pltpu.CompilerParams(collective_id=0, has_side_effects=True, vmem_limit_bytes=50 << 20),
        name="step",
    )(*args)


def write_kernel(*refs):
    sems = refs[-1]
    k = (len(refs) - 1) // 2
    copies = [pltpu.make_async_copy(refs[i], refs[k + i], sems.at[i]) for i in range(k)]
    for copy in copies:
        copy.start()
    for copy in copies:
        copy.wait()


def local(*args):
    n = lax.axis_size("dp")
    ids, lengths, dense, labels = args[:4]
    total_rows = ids.shape[0] * n
    params = [list(args[4 + 3 * k : 7 + 3 * k]) for k in range(9)]
    for k in (0, 5, 6):
        params[k] = [v.transpose(0, 2, 1) for v in params[k]]
    shapes = []
    for p in params:
        shapes += [(p[0].shape, F32)] * 3 + [(p[0].shape, BF)]
    shapes.append(((4,), F32))
    flat = [ids.transpose(1, 2, 0), lengths.T, dense.T, labels.T] + [v for p in params for v in p]
    results = step(flat, shapes, n, total_rows)
    results = [pltpu.with_memory_space_constraint(v, pltpu.VMEM) for v in results]
    outs = pl.pallas_call(
        write_kernel,
        out_shape=[jax.ShapeDtypeStruct(shape, dtype) for shape, dtype in shapes],
        in_specs=[pl.BlockSpec(memory_space=pltpu.VMEM)] * len(shapes),
        out_specs=[pl.BlockSpec(memory_space=pl.ANY)] * len(shapes),
        scratch_shapes=[pltpu.SemaphoreType.DMA((len(shapes),))],
        compiler_params=pltpu.CompilerParams(vmem_limit_bytes=1 << 20),
        name="write",
    )(*results)
    outs = list(outs)
    for k in (0, 5, 6):
        outs[4 * k : 4 * k + 4] = [v.transpose(0, 2, 1) for v in outs[4 * k : 4 * k + 4]]
    return tuple(outs)


def solution(mesh):
    up, down, bias = P(None, None, "hid"), P(None, "hid", None), P(None, "hid")
    rep = P()
    return jax.shard_map(
        local,
        mesh=mesh,
        in_specs=(P("dp", None, None), P("dp", None), P("dp", None), P("dp", None))
        + (rep,) * 6
        + (up,) * 3
        + (down,) * 3
        + (bias,) * 3
        + (rep,) * 12,
        out_specs=(rep,) * 8 + (up,) * 4 + (down,) * 4 + (bias,) * 4 + (rep,) * 17,
        check_vma=False,
    )
```

time: 93.1 us -> 82.9 us (0.89)
  Pallas kernels: 92 us -> 81.6 us
    pallas_call x2, Pallas kernels: 92 us -> 81.6 us  [the longest x1 77.6 us: step(): pl.pallas_call(functools.partial(step_kernel, n, chunks, total_rows, coun...]
where the time goes in v2:
time: 82.9 us; the launch traced here: 82.4 us
  Pallas kernels  81.6 us (98%)
  between operations  0.86 us (1%)
    pallas_call x1, Pallas kernels, step(): pl.pallas_call(functools.partial(step_kernel, n, chunks, total_rows, coun...  77.6 us
    pallas_call x1, Pallas kernels, local(): pl.pallas_call(write_kernel, out_shape=[jax.ShapeDtypeStruct(shape, dtype...  3.99 us

profile of v2, /device:TPU:0, one launch (start us, length us, event | category | flops | bytes accessed | tf_op | source)
XLA Modules:
  0.0 82.4 jit_solution(11408169093925280972)
XLA Ops:
  0.7 77.6 %step.1 = (f32[26,16,256]{2,1,0:T(8,128)S(1)}, f32[26,16,256]{2,1,0:T(8,128)S(1)}, f32[26,16,256]{2,1,0:T(8,128)S(1)}, bf16[26,16,256]{2,1,0:T(8,128)(2,1)S(1)},...) custom-call(s32[26,4,2048]{2,1,0:T(4,128)} %bitcast.25, ...), custom_call_target="tpu_custom_call" | custom-call | tf_op jit(solution)/shard_map/step/pallas_call | solution.py:736
  78.3 4.0 %write.1 = (f32[26,16,256]{2,1,0:T(8,128)}, f32[26,16,256]{2,1,0:T(8,128)}, f32[26,16,256]{2,1,0:T(8,128)}, bf16[26,16,256]{2,1,0:T(8,128)(2,1)}, f32[429,512]{1...) custom-call(f32[26,16,256]{2,1,0:T(8,128)S(1)} %get-tuple-element.11, ...), custom_call_target="tpu_custom_call" | custom-call | tf_op jit(solution)/shard_map/write/pallas_call | solution.py:771

commit v3 on v2

--- a/solution.py
+++ b/solution.py
@@ -41,55 +41,59 @@
 
 
 PARTS = (
-    ((640, "xyz"),),
-    ((640, "yxz"),),
     ((640, "pz"),),
+    ((256, "zyx"), (256, "zyx"), (128, "pz"),),
     ((640, "pz"),),
-    ((512, "pz"), (384, "zxy"),),
-    ((512, "pz"),),
+    ((256, "xyz"), (384, "yxz"),),
+    ((256, "zp"), (640, "pz"),),
+    ((256, "pz"), (256, "pz"),),
 )
 SCHEDULE = (
+    "!b0",
+    "!b3",
+    "!D0",
+    "!G0",
+    "e0a",
+    "!b1",
+    "!G1",
+    "e0a e1a e1b",
     "!b2",
-    "!b3",
+    "!D1",
+    "e1c e1a",
+    "!D2",
     "!G2",
-    "!D2",
-    "e2a",
+    "e2a e1c",
     "!G3",
-    "e2a",
+    "e1b e3a",
     "!D3",
-    "e3a",
-    "!b0",
-    "!b1",
-    "!G0",
-    "e3a",
-    "!D0",
-    "e0a",
-    "!G1",
-    "e0a",
-    "!D1",
-    "e1a",
-    "!s0",
-    "e2a e1a",
+    "e2a e3b",
     "!h0",
-    "e3a",
+    "e0a e3b e3a",
     "!i0",
     "e2a",
     "!i1",
-    "ib e1a ia e0a",
-    "!h1",
-    "ia ib",
-    "!j0-7",
-    "e1a e0a e2a",
-    "!j7-13",
-    "e3a ia ta ib",
-    "ta e1a e2a u2",
-    "ib e0a e3a ib",
-    "ia ta e1a e0a",
-    "ib ia e3a u3",
-    "ta e1a e0a ib",
-    "ia ta ia e1a",
-    "e0a u1 u0 ib",
-    "ib ui ta ta",
+    "ib e1b e1a ia",
+    "!s0",
+    "ib ia",
+    "!j0-8",
+    "e0a ta e3b e3a",
+    "!j8-10",
+    "e2a ta",
+    "!j10-13",
+    "tb e1b e1a e1c",
+    "ia ib e3a tb",
+    "e3b e0a e1b e1a",
+    "ta ia e2a e1c",
+    "tb ib e3a e3b",
+    "ta e1b e1a e0a",
+    "e1c u0 ia tb",
+    "ib e3a e1b e1a",
+    "e2a e3b u2 ta",
+    "e1c ia tb ia",
+    "ib e3a e3b ib",
+    "ui e1b ta ta",
+    "tb ut e3a e1a",
+    "tb u1 e3b u3",
     "ur",
 )
 
@@ -101,6 +105,10 @@
 
 def dot(a, b, dims):
     return lax.dot_general(a, b, dims, preferred_element_type=F32)
+
+
+def blocks(size, step=128):
+    return [slice(k, min(size, k + step)) for k in range(0, size, step)]
 
 
 def mm(a, b, dims=NN):
@@ -230,20 +238,15 @@
     sixteen = jnp.where(lax.broadcasted_iota(jnp.int32, (EMB, VOCAB), 1) < 128, 16.0, 1.0)
     width = 256
 
-    def pool_fields(i, carry):
-        for u in range(2):
-            f = 2 * i + u
-            table = jnp.concatenate(split(tab_ref[f] * sixteen), 0)
-            at = pl.ds(pl.multiple_of(EMB * f, EMB), EMB)
-            for j in range(rows // width):
-                here = slice(width * j, width * (j + 1))
-                both = dot(table, bag_counts(part, f, here, width), NN)
-                hi, lo = split(both[0:EMB] + both[EMB : 2 * EMB])
-                feat[0, at, here] = hi
-                feat[1, at, here] = lo
-        return carry
-
-    lax.fori_loop(0, FIELDS // 2, pool_fields, 0)
+    for f in range(FIELDS):
+        table = jnp.concatenate(split(tab_ref[f] * sixteen), 0)
+        at = slice(EMB * f, EMB * f + EMB)
+        for j in range(rows // width):
+            here = slice(width * j, width * (j + 1))
+            both = dot(table, bag_counts(part, f, here, width), NN)
+            hi, lo = split(both[0:EMB] + both[EMB : 2 * EMB])
+            feat[0, at, here] = hi
+            feat[1, at, here] = lo
     for load in loads[13:]:
         load.start()
 
@@ -303,6 +306,13 @@
     feat[0, POOLED:432, :] = hi
     feat[1, POOLED:432, :] = lo
 
+    scale = float(total_rows) ** -0.5
+    fs = (feat[0], feat[1])
+    xv = mm((w_in_t[0, :, 0:432], w_in_t[1, :, 0:432]), fs)
+    squares = [jnp.sum(xv * xv, keepdims=True)]
+    xs = split(xv)
+    x[0, 0:D, :] = xs[0]
+    x[1, 0:D, :] = xs[1]
     for copy in weights:
         copy.wait_recv()
     expert_weights(1, upx_ref, dnx_ref)
@@ -318,13 +328,6 @@
     cols[...] = bcol[...].T
     row_sums[...] = jnp.zeros((128, 128), F32)
 
-    scale = float(total_rows) ** -0.5
-    fs = (feat[0], feat[1])
-    xv = mm((w_in_t[0, :, 0:432], w_in_t[1, :, 0:432]), fs)
-    squares = [jnp.sum(xv * xv, keepdims=True)]
-    xs = split(xv)
-    x[0, 0:D, :] = xs[0]
-    x[1, 0:D, :] = xs[1]
     eouts, slopes = [], []
     sums = [0.0, 0.0, 0.0]
     for e in range(EXPERTS):
@@ -404,7 +407,6 @@
         bpu[1, c : c + 256, :] = bs[1]
 
     rep_base = chunks[EXPERTS][0][0]
-    sent = []
     used = {"sem": 0, "row": 0}
 
     def sems(count):
@@ -413,9 +415,10 @@
         return first
 
     class Piece:
-        def __init__(self, base, size, steps, expert):
-            self.base, self.size, self.expert = base, size, expert
+        def __init__(self, place, base, size, steps, expert):
+            self.place, self.base, self.size, self.expert = place, base, size, expert
             self.steps = [groups[k] for k in steps]
+            self.sent = 0
             self.plan = self.stages()
 
         def at(self, start, size):
@@ -426,30 +429,29 @@
                 return total_e.at[self.at(start, size)]
             return total_r.at[hid, self.at(start - rep_base, size)]
 
-        def start(self, copies):
-            for copy in copies:
-                copy.start()
-            sent.extend(copies)
-            return copies
+        def start(self, copies, rows):
+            k = sems(1)
+            for src, dst, peer in copies:
+                remote(src, dst, s_sem.at[self.place], v_sem.at[k], peer).start()
+            self.sent += rows
+            return remote(r_core.at[pl.ds(0, rows)], r_core.at[pl.ds(0, rows)], s_sem.at[self.place], v_sem.at[k], core_peer)
 
         def stages(self):
             rng = self.at(self.base, self.size)
-            k = sems(1)
-            yield self.start([remote(grads.at[1, rng], r_core.at[rng], s_sem.at[k], v_sem.at[k], core_peer)])
+            yield self.start([(grads.at[1, rng], r_core.at[rng], core_peer)], self.size)
             grads[0, rng, :] += r_core[rng, :]
             start, size, held = self.base, self.size, []
             for me, others in self.steps:
                 m = len(others) + 1
                 held.append((start, size))
                 size //= m
-                k, row = sems(m - 1), used["row"]
+                row = used["row"]
                 used["row"] += (m - 1) * size
                 copies = []
                 for j, (q, peer) in enumerate(others):
-                    slot = m - 2 - j
-                    src, dst = self.at(start + q * size, size), self.at(row + slot * size, size)
-                    copies.append(remote(grads.at[0, src], r_sum.at[dst], s_sem.at[k + j], v_sem.at[k + slot], peer))
-                yield self.start(copies)
+                    src, dst = self.at(start + q * size, size), self.at(row + (m - 2 - j) * size, size)
+                    copies.append((grads.at[0, src], r_sum.at[dst], peer))
+                yield self.start(copies, (m - 1) * size)
                 start = start + me * size
                 mine = self.at(start, size)
                 total = grads[0, mine, :]
@@ -460,28 +462,29 @@
                 else:
                     self.total(start, size)[...] = total
             for me, others in reversed(self.steps):
-                m = len(others) + 1
                 out = self.total(start, size)
-                k = sems(m - 1)
-                yield self.start(
-                    [remote(out, out, s_sem.at[k + j], v_sem.at[k + m - 2 - j], peer) for j, (_, peer) in enumerate(others)]
-                )
+                yield self.start([(out, out, peer) for _, peer in others], len(others) * size)
                 start, size = held.pop()
             if not self.expert:
                 out = self.total(self.base, self.size)
-                k = sems(1)
-                yield self.start([remote(out, out, s_sem.at[k], v_sem.at[k], core_peer)])
+                yield self.start([(out, out, core_peer)], self.size)
 
         def advance(self):
-            for copy in getattr(self, "copies", []):
-                copy.wait_recv()
-            self.copies = next(self.plan, [])
+            if self.step is not None:
+                self.step.wait_recv()
+            self.step = next(self.plan, None)
+
+        step = None
+
+        def end(self):
+            rows = pl.ds(0, self.sent)
+            remote(r_sum.at[rows], r_sum.at[rows], s_sem.at[self.place], v_sem.at[0], core_peer).wait_send()
 
     names = ("e0", "e1", "e2", "e3", "i", "t")
     pieces = {}
     for k, (name, parts) in enumerate(zip(names, chunks)):
         for j, (base, size, steps) in enumerate(parts):
-            pieces[name + "abcd"[j]] = Piece(base, size, steps, k < EXPERTS)
+            pieces[name + "abcd"[j]] = Piece(len(pieces), base, size, steps, k < EXPERTS)
 
     def owner(k):
         return (k + hid) % 2
@@ -587,15 +590,17 @@
             grads[:, base + E_ROWS : base + e_size, :] = jnp.zeros((2, e_size - E_ROWS, 128), F32)
 
     def inputs_back(k):
-        if k == 0:
-            b = mm((up_b[0], up_b[1]), (bpu[0], bpu[1])) + dot(gate_t[...], bgl[...], NN)
-            bs = split(b)
-            bi[0] = bs[0]
-            bi[1] = bs[1]
-        else:
-            ps = split(mm((w_in_b[0], w_in_b[1]), (bi[0], bi[1])))
-            bp[0] = ps[0]
-            bp[1] = ps[1]
+        parts = []
+        for at in blocks(D):
+            b = mm((up_b[0, at, :], up_b[1, at, :]), (bpu[0], bpu[1])) + dot(gate_t[at, :], bgl[...], NN)
+            parts.append(split(b))
+            bi[0, at, :] = parts[-1][0]
+            bi[1, at, :] = parts[-1][1]
+        bs = [jnp.concatenate([p[k] for p in parts], 0) for k in range(2)]
+        for at in blocks(POOLED):
+            ps = split(mm((w_in_b[0, at, :], w_in_b[1, at, :]), bs))
+            bp[0, at, :] = ps[0]
+            bp[1, at, :] = ps[1]
 
     def input_gradients(k):
         g = mm((feat[0], feat[1]), (bi[0, 256 * k : 256 * k + 256, :], bi[1, 256 * k : 256 * k + 256, :]), NT)
@@ -623,23 +628,18 @@
             total = jnp.where(lane == k, squares[k], total)
         grads[m, misc + 7 : misc + 8, :] = total
 
-    def table_fields(i, carry):
-        for u in range(2):
-            f = 2 * i + u
-            at = pl.ds(pl.multiple_of(EMB * f, EMB), EMB)
+    def tables(first, last):
+        for f in range(2 * first, 2 * last):
+            at = slice(EMB * f, EMB * f + EMB)
             total = jnp.zeros((2 * EMB, VOCAB), F32)
             for j in range(rows // width):
                 here = slice(width * j, width * (j + 1))
                 back = jnp.concatenate([bp[0, at, here], bp[1, at, here]], 0)
                 total = total + dot(back, bag_counts(part, f, here, width), NT)
             g = (total[0:EMB] + total[EMB : 2 * EMB]) * sixteen
-            at = pl.ds(pl.multiple_of(t_base + EMB * f, EMB), EMB)
+            at = slice(t_base + EMB * f, t_base + EMB * f + EMB)
             grads[owner(0), at, :] = g[:, 0:128]
             grads[owner(1), at, :] = g[:, 128:256]
-        return carry
-
-    def tables(first, last):
-        lax.fori_loop(first, last, table_fields, 0)
 
     work = {
         "b": expert_back,
@@ -656,11 +656,13 @@
             work[item[1]](int(item[2]))
         else:
             run(*item.split())
-    while any(piece.copies for piece in pieces.values()):
-        run(*[name for name in pieces if pieces[name].copies])
+    while any(piece.step for piece in pieces.values()):
+        run(*[name for name in pieces if pieces[name].step])
     run(*[name for name in updates if name not in done])
-    for copy in sent + weights:
+    for copy in weights:
         copy.wait_send()
+    for piece in pieces.values():
+        piece.end()
 
 
 def layout(n):
@@ -683,10 +685,10 @@
     rows = args[0].shape[2] // 2
     chunks, size = layout(n)
     e_all = chunks[EXPERTS][0][0]
-    count = 0
+    count, places = 0, sum(len(parts) for parts in chunks)
     for parts in chunks:
         for _, _, steps in parts:
-            count += 2 + 2 * sum({"x": 1, "y": 1, "p": 3, "z": n // 4 - 1, "a": n - 1}[k] for k in steps)
+            count += 2 + 2 * len(steps)
     vm = pltpu.VMEM
     scratch = [
         vm((FIELDS, 4, rows), jnp.int32),
@@ -729,7 +731,7 @@
         pltpu.SemaphoreType.DMA((31,)),
         pltpu.SemaphoreType.DMA((3,)),
         pltpu.SemaphoreType.DMA((3,)),
-        pltpu.SemaphoreType.DMA((count,)),
+        pltpu.SemaphoreType.DMA((places,)),
         pltpu.SemaphoreType.DMA((count,)),
     ]
     counts = [float(total_rows * c) for c in (D, EXPERTS * HID, EXPERTS * OUT, TASKS * TH)]

time: 82.9 us -> 77.5 us (0.935)
  Pallas kernels: 81.6 us -> 76 us
    pallas_call x1, Pallas kernels: 77.6 us -> 72.1 us  [step(): pl.pallas_call(functools.partial(step_kernel, n, chunks, total_rows, coun...]
where the time goes in v3:
time: 77.5 us; the launch traced here: 76.9 us
  Pallas kernels  76 us (98%)
  between operations  0.88 us (1%)
    pallas_call x1, Pallas kernels, step(): pl.pallas_call(functools.partial(step_kernel, n, chunks, total_rows, coun...  72.1 us
    pallas_call x1, Pallas kernels, local(): pl.pallas_call(write_kernel, out_shape=[jax.ShapeDtypeStruct(shape, dtype...  3.99 us

profile of v3, /device:TPU:0, one launch (start us, length us, event | category | flops | bytes accessed | tf_op | source)
XLA Modules:
  0.0 76.9 jit_solution(3952337768988427687)
XLA Ops:
  0.7 72.1 %step.1 = (f32[26,16,256]{2,1,0:T(8,128)S(1)}, f32[26,16,256]{2,1,0:T(8,128)S(1)}, f32[26,16,256]{2,1,0:T(8,128)S(1)}, bf16[26,16,256]{2,1,0:T(8,128)(2,1)S(1)},...) custom-call(s32[26,4,2048]{2,1,0:T(4,128)} %bitcast.25, ...), custom_call_target="tpu_custom_call" | custom-call | tf_op jit(solution)/shard_map/step/pallas_call | solution.py:738
  72.8 4.0 %write.1 = (f32[26,16,256]{2,1,0:T(8,128)}, f32[26,16,256]{2,1,0:T(8,128)}, f32[26,16,256]{2,1,0:T(8,128)}, bf16[26,16,256]{2,1,0:T(8,128)(2,1)}, f32[429,512]{1...) custom-call(f32[26,16,256]{2,1,0:T(8,128)S(1)} %get-tuple-element.11, ...), custom_call_target="tpu_custom_call" | custom-call | tf_op jit(solution)/shard_map/write/pallas_call | solution.py:773

commit v4 on v3

--- a/solution.py
+++ b/solution.py
@@ -1,4 +1,5 @@
 import functools
+import math
 
 import jax
 import jax.numpy as jnp
@@ -41,60 +42,54 @@
 
 
 PARTS = (
+    ((640, "zyx"),),
     ((640, "pz"),),
-    ((256, "zyx"), (256, "zyx"), (128, "pz"),),
     ((640, "pz"),),
-    ((256, "xyz"), (384, "yxz"),),
+    ((640, "pz"),),
     ((256, "zp"), (640, "pz"),),
     ((256, "pz"), (256, "pz"),),
 )
 SCHEDULE = (
+    "!b1",
     "!b0",
-    "!b3",
+    "!b2",
+    "!D2",
     "!D0",
+    "!D1",
+    "!G1",
+    "e1a",
     "!G0",
     "e0a",
-    "!b1",
-    "!G1",
-    "e0a e1a e1b",
-    "!b2",
-    "!D1",
-    "e1c e1a",
-    "!D2",
     "!G2",
-    "e2a e1c",
+    "e1a e2a",
+    "!b3",
+    "e0a",
     "!G3",
-    "e1b e3a",
     "!D3",
-    "e2a e3b",
+    "e3a e2a",
     "!h0",
-    "e0a e3b e3a",
+    "e1a e3a",
     "!i0",
-    "e2a",
     "!i1",
-    "ib e1b e1a ia",
+    "ib e2a ia",
     "!s0",
     "ib ia",
     "!j0-8",
-    "e0a ta e3b e3a",
+    "e1a ta e0a e3a",
     "!j8-10",
-    "e2a ta",
+    "ta",
     "!j10-13",
-    "tb e1b e1a e1c",
-    "ia ib e3a tb",
-    "e3b e0a e1b e1a",
-    "ta ia e2a e1c",
-    "tb ib e3a e3b",
-    "ta e1b e1a e0a",
-    "e1c u0 ia tb",
-    "ib e3a e1b e1a",
-    "e2a e3b u2 ta",
-    "e1c ia tb ia",
-    "ib e3a e3b ib",
-    "ui e1b ta ta",
-    "tb ut e3a e1a",
-    "tb u1 e3b u3",
-    "ur",
+    "tb e2a ia ib",
+    "tb e0a e1a ta",
+    "e3a ia e0a tb",
+    "e2a ib ta e1a",
+    "e0a ia e3a u1",
+    "tb ib e0a e2a",
+    "u2 ta ia tb",
+    "e3a u3 ia ib",
+    "ta ib ui ta",
+    "tb ut e0a u0",
+    "tb ur",
 )
 
 
@@ -195,7 +190,9 @@
     groups = {"x": group(1, 2), "y": group(2, 2), "z": group(4, n // 4), "p": group(1, 4), "a": group(1, n)}
 
     barrier = pltpu.get_barrier_semaphore()
-    everyone = [core_peer] + [peer for _, peer in groups["a"][1]]
+    kinds = {k for parts in chunks for _, _, steps in parts for k in steps}
+    kinds = ["a"] if "a" in kinds else ["p", "z"]
+    everyone = [core_peer] + [peer for k in kinds for _, peer in groups[k][1]]
     for peer in everyone:
         pl.semaphore_signal(barrier, inc=1, device_id=peer, device_id_type=MESH)
 
@@ -749,7 +746,8 @@
 def write_kernel(*refs):
     sems = refs[-1]
     k = (len(refs) - 1) // 2
-    copies = [pltpu.make_async_copy(refs[i], refs[k + i], sems.at[i]) for i in range(k)]
+    order = sorted(range(k), key=lambda i: -math.prod(refs[i].shape))
+    copies = [pltpu.make_async_copy(refs[i], refs[k + i], sems.at[i]) for i in order]
     for copy in copies:
         copy.start()
     for copy in copies:

time: 77.5 us -> 74.3 us (0.959)
  Pallas kernels: 76 us -> 73.3 us
    pallas_call x1, Pallas kernels: 72.1 us -> 69.3 us  [step(): pl.pallas_call(functools.partial(step_kernel, n, chunks, total_rows, coun...]
where the time goes in v4:
time: 74.3 us; the launch traced here: 74.2 us
  Pallas kernels  73.3 us (99%)
  between operations  0.88 us (1%)
    pallas_call x1, Pallas kernels, step(): pl.pallas_call(functools.partial(step_kernel, n, chunks, total_rows, coun...  69.3 us
    pallas_call x1, Pallas kernels, local(): pl.pallas_call(write_kernel, out_shape=[jax.ShapeDtypeStruct(shape, dtype...  3.97 us

profile of v4, /device:TPU:0, one launch (start us, length us, event | category | flops | bytes accessed | tf_op | source)
XLA Modules:
  0.0 74.2 jit_solution(3059388784917377450)
XLA Ops:
  0.7 69.3 %step.1 = (f32[26,16,256]{2,1,0:T(8,128)S(1)}, f32[26,16,256]{2,1,0:T(8,128)S(1)}, f32[26,16,256]{2,1,0:T(8,128)S(1)}, bf16[26,16,256]{2,1,0:T(8,128)(2,1)S(1)},...) custom-call(s32[26,4,2048]{2,1,0:T(4,128)} %bitcast.25, ...), custom_call_target="tpu_custom_call" | custom-call | tf_op jit(solution)/shard_map/step/pallas_call | solution.py:735
  70.0 4.0 %write.1 = (f32[26,16,256]{2,1,0:T(8,128)}, f32[26,16,256]{2,1,0:T(8,128)}, f32[26,16,256]{2,1,0:T(8,128)}, bf16[26,16,256]{2,1,0:T(8,128)(2,1)}, f32[429,512]{1...) custom-call(f32[26,16,256]{2,1,0:T(8,128)S(1)} %get-tuple-element.11, ...), custom_call_target="tpu_custom_call" | custom-call | tf_op jit(solution)/shard_map/write/pallas_call | solution.py:771

commit v5 on v4

--- a/solution.py
+++ b/solution.py
@@ -42,54 +42,56 @@
 
 
 PARTS = (
-    ((640, "zyx"),),
     ((640, "pz"),),
     ((640, "pz"),),
-    ((640, "pz"),),
-    ((256, "zp"), (640, "pz"),),
+    ((640, "zxy"),),
+    ((640, "xyz"),),
+    ((384, "pz"), (512, "pz"),),
     ((256, "pz"), (256, "pz"),),
 )
 SCHEDULE = (
     "!b1",
     "!b0",
     "!b2",
-    "!D2",
-    "!D0",
+    "!b3",
+    "!G1",
     "!D1",
-    "!G1",
     "e1a",
     "!G0",
+    "!D0",
+    "e1a e0a",
+    "!G2",
+    "!D2",
+    "e2a",
+    "!G3",
     "e0a",
-    "!G2",
-    "e1a e2a",
-    "!b3",
-    "e0a",
-    "!G3",
     "!D3",
     "e3a e2a",
     "!h0",
-    "e1a e3a",
+    "e3a",
+    "!h1",
     "!i0",
     "!i1",
-    "ib e2a ia",
+    "ib e1a ia",
+    "!h2",
+    "ib e0a",
     "!s0",
-    "ib ia",
+    "e3a",
     "!j0-8",
-    "e1a ta e0a e3a",
-    "!j8-10",
-    "ta",
-    "!j10-13",
-    "tb e2a ia ib",
-    "tb e0a e1a ta",
-    "e3a ia e0a tb",
-    "e2a ib ta e1a",
-    "e0a ia e3a u1",
-    "tb ib e0a e2a",
-    "u2 ta ia tb",
-    "e3a u3 ia ib",
-    "ta ib ui ta",
-    "tb ut e0a u0",
-    "tb ur",
+    "e1a ta e2a ia",
+    "e0a",
+    "!j8-13",
+    "ta tb ib e3a",
+    "e2a tb e1a ia",
+    "ta e2a e0a ib",
+    "tb e3a ia ta",
+    "e2a e1a u1 ib",
+    "tb e3a e2a e0a",
+    "ia u0 ta tb",
+    "ib e3a ib ia",
+    "ia ta ui ta",
+    "tb ut e2a tb",
+    "u2 ur e3a u3",
 )
 
 
@@ -213,14 +215,6 @@
             src_ref=src, dst_ref=dst, send_sem=send, recv_sem=recv, device_id=peer, device_id_type=MESH
         )
 
-    pl.semaphore_wait(barrier, len(everyone))
-    weights = [
-        remote(src, dst, w_send.at[k], w_recv.at[k], core_peer)
-        for k, (src, dst) in enumerate(((up_hbm, upx_ref), (dn_hbm, dnx_ref), (upb_hbm, upbx_ref)))
-    ]
-    for copy in weights:
-        copy.start()
-
     loads[0].wait()
     loads[1].wait()
     slot = lax.broadcasted_iota(jnp.int32, (4, rows), 0)
@@ -229,13 +223,12 @@
         ident = ids_ref[f]
         part[0, f] = jnp.where(used, jnp.where(ident < 128, 0.0625, 1.0), 0.0)
         part[1, f] = jnp.bitwise_and(ident, 127).astype(F32)
-    for load in loads[2:13]:
-        load.wait()
+    loads[2].wait()
 
     sixteen = jnp.where(lax.broadcasted_iota(jnp.int32, (EMB, VOCAB), 1) < 128, 16.0, 1.0)
     width = 256
 
-    for f in range(FIELDS):
+    def pool_field(f):
         table = jnp.concatenate(split(tab_ref[f] * sixteen), 0)
         at = slice(EMB * f, EMB * f + EMB)
         for j in range(rows // width):
@@ -244,8 +237,22 @@
             hi, lo = split(both[0:EMB] + both[EMB : 2 * EMB])
             feat[0, at, here] = hi
             feat[1, at, here] = lo
+
+    for f in range(13):
+        pool_field(f)
+    pl.semaphore_wait(barrier, len(everyone))
+    weights = [
+        remote(src, dst, w_send.at[k], w_recv.at[k], core_peer)
+        for k, (src, dst) in enumerate(((up_hbm, upx_ref), (dn_hbm, dnx_ref), (upb_hbm, upbx_ref)))
+    ]
+    for copy in weights:
+        copy.start()
+    for f in range(13, FIELDS):
+        pool_field(f)
     for load in loads[13:]:
         load.start()
+    for load in loads[3:13]:
+        load.wait()
 
     brow[0:1, 0:1024] = bias_ref[0:1024].reshape(1, 1024)
     brow[0:1, 1024:NB] = bias_ref[1024:NB].reshape(1, NB - 1024)
@@ -586,14 +593,17 @@
         if e_size > E_ROWS:
             grads[:, base + E_ROWS : base + e_size, :] = jnp.zeros((2, e_size - E_ROWS, 128), F32)
 
+    inputs_parts = []
+
     def inputs_back(k):
-        parts = []
-        for at in blocks(D):
-            b = mm((up_b[0, at, :], up_b[1, at, :]), (bpu[0], bpu[1])) + dot(gate_t[at, :], bgl[...], NN)
-            parts.append(split(b))
-            bi[0, at, :] = parts[-1][0]
-            bi[1, at, :] = parts[-1][1]
-        bs = [jnp.concatenate([p[k] for p in parts], 0) for k in range(2)]
+        if k < 2:
+            for at in blocks(D)[2 * k : 2 * k + 2]:
+                b = mm((up_b[0, at, :], up_b[1, at, :]), (bpu[0], bpu[1])) + dot(gate_t[at, :], bgl[...], NN)
+                inputs_parts.append(split(b))
+                bi[0, at, :] = inputs_parts[-1][0]
+                bi[1, at, :] = inputs_parts[-1][1]
+            return
+        bs = [jnp.concatenate([p[j] for p in inputs_parts], 0) for j in range(2)]
         for at in blocks(POOLED):
             ps = split(mm((w_in_b[0, at, :], w_in_b[1, at, :]), bs))
             bp[0, at, :] = ps[0]

time: 74.3 us -> 73.3 us (0.987)
  Pallas kernels: 73.3 us -> 71.9 us
    pallas_call x1, Pallas kernels: 69.3 us -> 67.9 us  [step(): pl.pallas_call(functools.partial(step_kernel, n, chunks, total_rows, coun...]
where the time goes in v5:
time: 73.3 us; the launch traced here: 72.8 us
  Pallas kernels  71.9 us (98%)
  between operations  0.88 us (1%)
    pallas_call x1, Pallas kernels, step(): pl.pallas_call(functools.partial(step_kernel, n, chunks, total_rows, coun...  67.9 us
    pallas_call x1, Pallas kernels, local(): pl.pallas_call(write_kernel, out_shape=[jax.ShapeDtypeStruct(shape, dtype...  3.97 us

profile of v5, /device:TPU:0, one launch (start us, length us, event | category | flops | bytes accessed | tf_op | source)
XLA Modules:
  0.0 72.8 jit_solution(1290728071831799478)
XLA Ops:
  0.7 67.9 %step.1 = (f32[26,16,256]{2,1,0:T(8,128)S(1)}, f32[26,16,256]{2,1,0:T(8,128)S(1)}, f32[26,16,256]{2,1,0:T(8,128)S(1)}, bf16[26,16,256]{2,1,0:T(8,128)(2,1)S(1)},...) custom-call(s32[26,4,2048]{2,1,0:T(4,128)} %bitcast.25, ...), custom_call_target="tpu_custom_call" | custom-call | tf_op jit(solution)/shard_map/step/pallas_call | solution.py:745
  68.6 4.0 %write.1 = (f32[26,16,256]{2,1,0:T(8,128)}, f32[26,16,256]{2,1,0:T(8,128)}, f32[26,16,256]{2,1,0:T(8,128)}, bf16[26,16,256]{2,1,0:T(8,128)(2,1)}, f32[429,512]{1...) custom-call(f32[26,16,256]{2,1,0:T(8,128)S(1)} %get-tuple-element.11, ...), custom_call_target="tpu_custom_call" | custom-call | tf_op jit(solution)/shard_map/write/pallas_call | solution.py:781
